TPU v7x, 256 devices: a whole 4x4x8 slice. The times are simulated.
256 devices in a mesh: seq: 16 (over z_lo, x), ri: 4 (over z_hi, core), rj: 4 (over y).
Axes of the slice: x: 4, y: 4, z: 8 (z_hi: 2, z_lo: 4; z = z_hi * 4 + z_lo), core: 2. Of those that a mesh axis runs over, the one named last changes fastest.
Arguments:
- homolog_embedding: bfloat16 [256, 512, 256], P('seq', 'ri'), may hold values from -6 to 6
- pairwise_state: bfloat16 [512, 512, 128], P('ri', ('seq', 'rj')), may hold values from -6 to 6
- residue_mask: int32 [512], replicated, may hold values 0 or 1
- alignment_row_mask: int32 [256], replicated, may hold values 0 or 1
- focus_layer_scale: float32 [256], replicated, may hold values from 0.25 to 1.75
- asking_projector: bfloat16 [256, 256], P(None, 'rj'), may hold values from -1 to 1
- lookup_projector: bfloat16 [256, 256], P(None, 'rj'), may hold values from -1 to 1
- content_projector: bfloat16 [256, 256], P(None, 'rj'), may hold values from -0.375 to 0.375
- sigmoid_projector: bfloat16 [256, 256], P(None, 'rj'), may hold values from -0.375 to 0.375
- gate_offset_bias: float32 [256], replicated, may hold values from -4 to 4
- final_projector: bfloat16 [256, 256], P('rj'), may hold values from -1.5 to 1.5
- pairwise_norm_gain: float32 [128], replicated, may hold values from 0.25 to 1.75
- bias_weight: bfloat16 [128, 8], replicated, may hold values from -5 to 5
- cross_layer_scale: float32 [256], replicated, may hold values from 0.25 to 1.75
- first_cross_projector: bfloat16 [256, 32], replicated, may hold values from -0.375 to 0.375
- second_cross_projector: bfloat16 [256, 32], replicated, may hold values from -0.375 to 0.375
- outer_weight: bfloat16 [1024, 128], replicated, may hold values from -3 to 3
Outputs:
- alignment_output: bfloat16 [256, 512, 256], P('seq', 'ri')
- pairwise_output: bfloat16 [512, 512, 128], P('ri', ('seq', 'rj'))
All inputs are finite; a program needn't handle non-finite values.
Results may differ from a plain program's by a relative error of at most 0.015.
The roundings to bfloat16 on the way count: a program that leaves them out, or rounds other values in their place, can miss the bound.
Values may be sent and summed in bfloat16 or wider, within the bound.
A program may use at most 64 MiB of HBM per device.

v0:
```python
import jax
import jax.numpy as jnp
from jax import lax
from jax.sharding import PartitionSpec as P

SPLIT_DEPTH = 32
CROSS_FEATURES = 32


def normed_rows(values, gain):
    values = values.astype(jnp.float32)
    centre = values - jnp.mean(values, -1, keepdims=True)
    spread = jnp.mean(centre * centre, -1, keepdims=True)
    return centre * lax.rsqrt(spread + 1e-05) * gain


def on_device(
    homolog_embedding,
    pairwise_state,
    residue_mask,
    alignment_row_mask,
    focus_layer_scale,
    asking_projector,
    lookup_projector,
    content_projector,
    sigmoid_projector,
    gate_offset_bias,
    final_projector,
    pairwise_norm_gain,
    bias_weight,
    cross_layer_scale,
    first_cross_projector,
    second_cross_projector,
    outer_weight,
):
    highest = lax.Precision.HIGHEST
    sequences_local, residue_block, channel_count = homolog_embedding.shape
    tile_rows, tile_cols, pair_width = pairwise_state.shape
    local_heads = asking_projector.shape[1] // SPLIT_DEPTH
    seq_count = lax.axis_size("seq")
    col_count = lax.axis_size("rj")
    rj_index = lax.axis_index("rj")
    res_float = residue_mask.astype(jnp.float32)
    row_float = alignment_row_mask.astype(jnp.float32)
    query_weight_local, key_weight_local, value_weight_local, gate_weight_local, weight_o = (
        asking_projector,
        lookup_projector,
        content_projector,
        sigmoid_projector,
        final_projector,
    )
    local_bias = lax.dynamic_slice_in_dim(
        gate_offset_bias, rj_index * local_heads * SPLIT_DEPTH, local_heads * SPLIT_DEPTH, 0
    )
    alignment_normed = normed_rows(homolog_embedding, focus_layer_scale).astype(jnp.bfloat16)
    query_matrix = (
        jnp.dot(alignment_normed, query_weight_local, preferred_element_type=jnp.float32)
        * SPLIT_DEPTH ** (-0.5)
    ).astype(jnp.bfloat16)
    key_matrix = jnp.dot(
        alignment_normed, key_weight_local, preferred_element_type=jnp.float32
    ).astype(jnp.bfloat16)
    value_matrix = jnp.dot(
        alignment_normed, value_weight_local, preferred_element_type=jnp.float32
    ).astype(jnp.bfloat16)
    gate_values = jax.nn.sigmoid(
        jnp.dot(alignment_normed, gate_weight_local, preferred_element_type=jnp.float32)
        + local_bias
    )
    pair_norm = normed_rows(pairwise_state, pairwise_norm_gain).astype(jnp.bfloat16)
    bias_tile = jnp.einsum(
        "rcz,zh->hrc", pair_norm, bias_weight, preferred_element_type=jnp.float32
    ).astype(jnp.bfloat16)
    bias_full = lax.all_gather(bias_tile, ("seq", "rj"), axis=2, tiled=True)
    bias_rows = lax.dynamic_slice_in_dim(bias_full, rj_index * local_heads, local_heads, 0)
    query_four = query_matrix.reshape(sequences_local, residue_block, local_heads, SPLIT_DEPTH)
    key_bias = 1000000000.0 * (res_float - 1.0)
    running_max = jnp.full((sequences_local, local_heads, residue_block), -1e30, jnp.float32)
    key_piece = lax.all_gather(key_matrix, "ri", axis=1, tiled=True)
    value_piece = lax.all_gather(value_matrix, "ri", axis=1, tiled=True)
    width = key_piece.shape[1]
    key_four = key_piece.reshape(sequences_local, width, local_heads, SPLIT_DEPTH)
    value_four = value_piece.reshape(sequences_local, width, local_heads, SPLIT_DEPTH).astype(
        jnp.float32
    )
    logits = jnp.einsum("sihd,sjhd->shij", query_four, key_four, preferred_element_type=jnp.float32)
    logits = logits + bias_rows.astype(jnp.float32)[None]
    logits = logits + key_bias[None, None, None, :]
    new_max = jnp.maximum(running_max, jnp.max(logits, -1))
    weights = jnp.exp(logits - new_max[..., None])
    running_sum = jnp.sum(weights, -1)
    running_out = jnp.einsum("shij,sjhd->shid", weights, value_four, precision=highest)
    heads_out = (
        (running_out / running_sum[..., None])
        .transpose(0, 2, 1, 3)
        .reshape(sequences_local, residue_block, local_heads * SPLIT_DEPTH)
    )
    attended_values = (heads_out * gate_values).astype(jnp.bfloat16)
    partial_out = jnp.dot(attended_values, weight_o, preferred_element_type=jnp.float32)
    summed_output = lax.psum(partial_out, "rj")
    alignment_output = (homolog_embedding.astype(jnp.float32) + summed_output).astype(jnp.bfloat16)
    product_normed = normed_rows(alignment_output, cross_layer_scale).astype(jnp.bfloat16)
    row_here = lax.dynamic_slice_in_dim(
        row_float, lax.axis_index("seq") * sequences_local, sequences_local, 0
    )
    res_here = lax.dynamic_slice_in_dim(
        res_float, lax.axis_index("ri") * residue_block, residue_block, 0
    )
    weight_mask = (row_here[:, None] * res_here[None, :])[:, None, :]
    left = (
        jnp.einsum(
            "src,ck->skr", product_normed, first_cross_projector, preferred_element_type=jnp.float32
        )
        * weight_mask
    ).astype(jnp.bfloat16)
    right = (
        jnp.einsum(
            "src,ck->skr",
            product_normed,
            second_cross_projector,
            preferred_element_type=jnp.float32,
        )
        * weight_mask
    ).astype(jnp.bfloat16)
    right_every_res = lax.all_gather(right, "ri", axis=2, tiled=True)
    right_split = right_every_res.reshape(
        sequences_local, CROSS_FEATURES, seq_count, col_count, tile_cols
    )
    right_picked = lax.dynamic_slice_in_dim(right_split, rj_index, 1, 3).reshape(
        sequences_local, CROSS_FEATURES, seq_count, tile_cols
    )
    w_cube = outer_weight.astype(jnp.float32).reshape(CROSS_FEATURES, CROSS_FEATURES, pair_width)
    right_flat = right_picked.reshape(sequences_local, CROSS_FEATURES, seq_count * tile_cols)
    amount = tile_cols * lax.axis_size("seq")
    groups = amount // tile_cols
    grouped = right_flat.reshape(sequences_local, CROSS_FEATURES, groups, tile_cols).transpose(
        2, 0, 1, 3
    )

    def one_group(column_block):
        outer_part = jnp.einsum(
            "ski,slc->cikl", left, column_block, preferred_element_type=jnp.float32
        )
        return jnp.einsum("cikl,klz->ciz", outer_part, w_cube, precision=highest)

    summed_cols = lax.psum_scatter(
        lax.map(one_group, grouped).reshape(amount, residue_block, pair_width),
        "seq",
        scatter_dimension=0,
        tiled=True,
    )
    update = summed_cols.transpose(1, 0, 2)
    col_start = (lax.axis_index("seq") * col_count + rj_index) * tile_cols
    res_cols = lax.dynamic_slice_in_dim(res_float, col_start, tile_cols, 0)
    row_total = jnp.sum(row_float)
    divisor = jnp.maximum(res_here[:, None] * res_cols[None, :] * row_total, 1.0)
    pairwise_output = (pairwise_state.astype(jnp.float32) + update / divisor[:, :, None]).astype(
        jnp.bfloat16
    )
    return (alignment_output, pairwise_output)


def solution(mesh):
    placed = (
        P("seq", "ri", None),
        P("ri", ("seq", "rj"), None),
        P(),
        P(),
        P(),
        P(None, "rj"),
        P(None, "rj"),
        P(None, "rj"),
        P(None, "rj"),
        P(),
        P("rj", None),
        P(),
        P(),
        P(),
        P(),
        P(),
        P(),
    )
    return jax.shard_map(
        on_device,
        mesh=mesh,
        in_specs=placed,
        out_specs=(P("seq", "ri", None), P("ri", ("seq", "rj"), None)),
        check_vma=False,
    )
```

profile of v0, /device:TPU:16, one launch (start us, length us, event | category | flops | bytes accessed | tf_op | source)
XLA Modules:
  0.0 788.3 jit_solution(7447958525760588368)
XLA Ops:
  18.0 342.5 %all-gather.6.cloned.1.call-done = bf16[8,128,512]{1,0,2:T(8,128)(2,1)} async-done(((bf16[8,128,8]{1,0,2:T(8,128)(2,1)}), bf16[8,128,512]{1,0,2:T(8,128)(2,1)}) %all-gather.6.cloned.1.call-update) | async-done | bytes 1048592 | tf_op jit(solution)/shard_map/all_gather | solution.py:74
  362.2 31.7 %all-gather.4.cloned.1.call-done = bf16[16,512,64]{1,2,0:T(8,128)(2,1)} async-done(((bf16[16,128,64]{1,2,0:T(8,128)(2,1)}), bf16[16,512,64]{1,2,0:T(8,128)(2,1)}) %all-gather.4.cloned.1.call-update) | async-done | bytes 1048592 | tf_op jit(solution)/shard_map/all_gather | solution.py:79
  402.2 22.1 %all-gather.8.cloned.1.call-done = bf16[16,512,64]{1,2,0:T(8,128)(2,1)} async-done(((bf16[16,128,64]{1,2,0:T(8,128)(2,1)}), bf16[16,512,64]{1,2,0:T(8,128)(2,1)}) %all-gather.8.cloned.1.call-update) | async-done | bytes 1048592 | tf_op jit(solution)/shard_map/all_gather | solution.py:80
  424.4 9.5 %fusion.33 = f32[16,128,2,32]{1,3,2,0:T(8,128)S(1)} fusion(bf16[16,512,2,32]{1,3,2,0:T(8,128)(2,1)} %bitcast.91, f32[16,2,128,512]{3,2,1,0:T(8,128)} %copy-done.1, f32[16,2,128]{2,1,0:T(2,128)S(1)} %broadcast_maximum_fusion, f32[512]{0:T(512)S(1)} %add_multiply_fusion, f32[2,128,512]{2,1,0:T(8,128)S(1)} %convert_element_type.75, f32[16,128,2]{1,2,0:T(2,128)S(1)} %bitcast.90), kind=kOutput, calls=%fused_computation.46 | convolution fusion | flops 811728896 | bytes 10520576 | tf_op jit(solution)/shard_map/shij,sjhd->shid/dot_general | solution.py:92
  438.4 56.7 %all-reduce.2.cloned.1.call-done = f32[16,128,256]{2,1,0:T(8,128)} async-done(((f32[16,128,256]{2,1,0:T(8,128)}), f32[16,128,256]{2,1,0:T(8,128)}) %all-reduce.2.cloned.1.call-update) | async-done | bytes 2097168 | tf_op jit(solution)/shard_map/psum | solution.py:100
  499.7 11.7 %all_gather.15 = bf16[16,32,512]{2,1,0:T(8,128)(2,1)S(1)} all-gather(bf16[16,32,128]{2,1,0:T(8,128)(2,1)S(1)} %fusion.39), channel_id=1, replica_groups=mesh['seq'=16,'ri'=4,'rj'=4] {'ri'}, dimensions={2}, use_global_device_ids=true | all-gather | bytes 655360 | tf_op jit(solution)/shard_map/all_gather | solution.py:125
  513.5 156.8 %while.10 = (s32[]{:T(128)}, f32[16,8,128,128]{3,1,0,2:T(8,128)}, bf16[16,16,32,8]{2,3,0,1:T(8,128)(2,1)}, bf16[16,32,128]{2,0,1:T(8,128)(2,1)S(1)}, f32[32,32,128]{2,1,0:T(8,128)}, /*index=5*/s32[]{:T(128)}) while((s32[]{:T(128)}, f32[16,8,128,128]{3,1,0,2:T(8,128)}, bf16[16,16,32,8]{2,3,0,1:T(8,128)(2,1)}, ...), condition=%wide.region_10.11_spmd, body=%wide.region_9.10_spmd.sunk | while | flops 1644167168 | bytes 12739173 | solution.py:147
  515.3 6.8 fusion.82
  525.1 6.8 fusion.82
  534.8 6.8 fusion.82
  544.6 6.8 fusion.82
  554.5 6.8 fusion.82
  564.2 6.8 fusion.82
  574.0 6.8 fusion.82
  583.8 6.8 fusion.82
  593.6 6.8 fusion.82
  603.5 6.8 fusion.82
  613.2 6.8 fusion.82
  623.0 6.8 fusion.82
  632.8 6.8 fusion.82
  642.6 6.8 fusion.82
  652.4 6.8 fusion.82
  662.3 6.8 fusion.82
  671.8 108.0 %reduce-scatter.2.cloned.1.call-done = f32[8,128,128]{2,0,1:T(8,128)} async-done(((f32[128,128,128]{2,0,1:T(8,128)}), f32[8,128,128]{2,0,1:T(8,128)}) %reduce-scatter.2.cloned.1.call-update) | async-done | bytes 524304 | tf_op jit(solution)/shard_map/reduce_scatter | solution.py:146
  (167 shorter events, 82.5 us)
Async XLA Ops:
  7.2 426.7 %copy-start = (bf16[64,256]{1,0:T(8,128)(2,1)S(1)}, bf16[64,256]{1,0:T(8,128)(2,1)}, u32[]{:S(2)}) copy-start(bf16[64,256]{1,0:T(8,128)(2,1)} %param.29) | copy-start | bytes 98308
  7.2 5.0 copy-start.2
  7.2 353.3 %all-gather.6.cloned.1.call-start = ((), (), s32[]{:S(2)}) async-start(), calls=%async_computation.2 | async-start | bytes 1064960 | tf_op jit(solution)/shard_map/all_gather | solution.py:74
  9.8 3.3 copy-start.9
  9.9 3.3 copy-start.16
  12.1 381.8 %all-gather.4.cloned.1.call-start = ((), (), s32[]{:S(2)}) async-start(), calls=%async_computation.1 | async-start | bytes 1310720 | tf_op jit(solution)/shard_map/all_gather | solution.py:79
  12.5 2.5 copy-start.10
  14.9 2.0 copy-start.11
  14.9 3.0 copy-start.7
  14.9 3.0 copy-start.15
  14.9 409.4 %all-gather.8.cloned.1.call-start = ((), (), s32[]{:S(2)}) async-start(), calls=%async_computation.3 | async-start | bytes 1310720 | tf_op jit(solution)/shard_map/all_gather | solution.py:80
  16.7 478.4 %all-reduce.2.cloned.1.call-start = ((), (), s32[]{:S(2)}) async-start(), calls=%async_computation.4 | async-start | bytes 4194304 | tf_op jit(solution)/shard_map/psum | solution.py:100
  396.7 3.2 copy-start.1
  424.4 9.5 %copy-start.12 = (bf16[256,64]{0,1:T(8,128)(2,1)S(1)}, bf16[256,64]{0,1:T(8,128)(2,1)}, u32[]{:S(2)}) copy-start(bf16[256,64]{0,1:T(8,128)(2,1)} %param.27) | copy-start | bytes 98308
  436.3 343.4 %reduce-scatter.2.cloned.1.call-start = ((), (), s32[]{:S(2)}) async-start(), calls=%async_computation.5 | async-start | bytes 8912896 | tf_op jit(solution)/shard_map/reduce_scatter | solution.py:146
  438.4 59.3 %copy-start.13 = (bf16[256,32]{0,1:T(8,128)(2,1)S(1)}, bf16[256,32]{0,1:T(8,128)(2,1)}, u32[]{:S(2)}) copy-start(bf16[256,32]{0,1:T(8,128)(2,1)} %param.33) | copy-start | bytes 49156
  438.4 59.3 %copy-start.17 = (f32[256]{0:T(256)S(1)}, f32[256]{0:T(256)}, u32[]{:S(2)}) copy-start(f32[256]{0:T(256)} %param.32) | copy-start | bytes 3076
  497.0 2.7 copy-start.3
  497.0 1.7 copy-start.14
  514.2 1.0 copy-start.5
  524.0 1.0 copy-start.5
  533.8 1.0 copy-start.5
  543.6 1.0 copy-start.5
  670.2 109.5 %copy-start.4 = (bf16[128,8,128]{2,1,0:T(8,128)(2,1)S(1)}, bf16[128,8,128]{2,1,0:T(8,128)(2,1)}, u32[]{:S(2)}) copy-start(bf16[128,8,128]{2,1,0:T(8,128)(2,1)} %param.20) | copy-start | bytes 786436
  (14 other events, 14.1 us)
Sparse Core Ops, SparseCore 0:
  12.2 348.2 all-gather.5
  362.9 30.9 all-gather.3
  396.3 27.9 all-gather.7
  436.5 58.5 all-reduce.1
  670.4 109.3 reduce-scatter.1
where the time goes:
time: 791 us; the launch traced here: 788 us
  waiting for transfers between devices  561 us (71%)
  matrix products  143 us (18%)
  local copies, waits for them, and re-layouts  44.8 us (6%)
  between operations  14.2 us (2%)
  other arithmetic  12.7 us (2%)
  blocking collectives  11.7 us (1%)
    all_gather x1, waiting for transfers between devices, on_device(): bias_full = lax.all_gather(bias_tile, ('seq', 'rj'), axis=2, tiled=True)  342 us
    dot_general x16, matrix products, one_group(): return jnp.einsum('cikl,klz->ciz', outer_part, w_cube, precision=highest)  109 us
    reduce_scatter x1, waiting for transfers between devices, on_device(): lax.psum_scatter(lax.map(one_group, grouped).reshape(amount, residue_bloc...  108 us
    psum x1, waiting for transfers between devices, on_device(): summed_output = lax.psum(partial_out, 'rj')  56.7 us
    all_gather x1, waiting for transfers between devices, on_device(): key_piece = lax.all_gather(key_matrix, 'ri', axis=1, tiled=True)  31.7 us
    all_gather x1, waiting for transfers between devices, on_device(): value_piece = lax.all_gather(value_matrix, 'ri', axis=1, tiled=True)  22.1 us
    dynamic_update_slice x16, local copies, waits for them, and re-layouts, on_device(): lax.map(one_group, grouped).reshape(amount, residue_block, pair_width)  18.6 us
  transfers between devices with their start and end apart: 5, of which 5 were waited for; matrix products, arithmetic and copies ran while one was open for 2% of the time, Pallas kernels for 0%

commit v1 on v0

v1 whole, which is shorter than its diff:
```python
import jax
import jax.numpy as jnp
from jax import lax
from jax.experimental import pallas as pl
from jax.experimental.pallas import tpu as pltpu
from jax.sharding import PartitionSpec as P

F32 = jnp.float32
BF = jnp.bfloat16
NT = (((1,), (1,)), ((), ()))

XZ, XM, XF = 0, 4, 8
WT, BZ, BY, BX = 12, 15, 18, 21
AL, A2 = 24, 36
LZ, LX = 39, 42
R2, R4 = 54, 58
UP = 70
COUNT = 73


def nt(a, b):
    return lax.dot_general(a, b, NT, preferred_element_type=F32)


def mm(a, b):
    return jnp.dot(a, b, preferred_element_type=F32)


def norm(values, gain):
    centre = values - jnp.mean(values, -1, keepdims=True)
    spread = jnp.mean(centre * centre, -1, keepdims=True)
    return centre * lax.rsqrt(spread + 1e-5) * gain


def eye(n):
    row = lax.broadcasted_iota(jnp.int32, (n, n), 0)
    col = lax.broadcasted_iota(jnp.int32, (n, n), 1)
    return (row == col).astype(F32).astype(BF)


def kernel(
    hom, pair, resm, rows, rowv, fscale, wq, wk, wv, wg, gb, wo, pgain, bw, cscale, p1, p2, ow,
    out_al, out_pair,
    xin, xn, wbuf, pn, bt, bg, biasf, gbt, cm, wst, al, sndf, snd, rcv, scr, lb, rst, rb,
    bscr, ub, ubf, urecv,
    ssem, rsem, xsem, osem,
):
    seq = lax.axis_index("seq")
    ri = lax.axis_index("ri")
    rj = lax.axis_index("rj")
    zl, x = lax.div(seq, 4), lax.rem(seq, 4)
    mate = ri + 1 - 2 * lax.rem(ri, 2)
    opp = lax.rem(ri + 2, 4)
    oppmate = lax.rem(mate + 2, 4)

    def ahead(v, d):
        return lax.rem(v + d, 4)

    def behind(v, d):
        return lax.rem(v + 4 - d, 4)

    ypeer = [{"rj": ahead(rj, d)} for d in (1, 2, 3)]
    xpeer = [{"seq": zl * 4 + ahead(x, d)} for d in (1, 2, 3)]
    zpeer = [{"seq": ahead(zl, d) * 4 + x} for d in (1, 2, 3)]
    rdest = [{"seq": ri * 4 + rj, "ri": t, "rj": x} for t in range(4)]
    rsrc = [{"seq": t * 4 + rj, "ri": zl, "rj": x} for t in range(4)]
    diagonal = jnp.logical_and(zl == ri, x == rj)

    def rcopy(src, dst, k, dev, send=None):
        return pltpu.make_async_remote_copy(
            src_ref=src,
            dst_ref=dst,
            send_sem=ssem.at[k if send is None else send],
            recv_sem=rsem.at[k],
            device_id=dev,
            device_id_type=pl.DeviceIdType.MESH,
        )

    def arrived(ref, k):
        pltpu.make_async_copy(ref, ref, rsem.at[k]).wait()

    def left_here(ref, k):
        pltpu.make_async_copy(ref, ref, ssem.at[k]).wait()

    barrier = pltpu.get_barrier_semaphore()

    def greet(dev):
        pl.semaphore_signal(barrier, inc=1, device_id=dev, device_id_type=pl.DeviceIdType.MESH)

    for dev in ypeer + xpeer + zpeer + [{"ri": mate}, {"ri": opp}]:
        greet(dev)
    for t in range(4):

        @pl.when(jnp.logical_not(jnp.logical_and(diagonal, ri == t)))
        def _():
            greet(rdest[t])

        @pl.when(jnp.logical_not(jnp.logical_and(diagonal, zl == t)))
        def _():
            greet(rsrc[t])

    xcopy = pltpu.make_async_copy(hom.at[pl.ds(rj * 4, 4)], xin, xsem)
    xcopy.start()

    pn[...] = norm(pair[...].astype(F32), pgain[...]).astype(BF).astype(F32)
    bwt = bw[...]
    for j in range(8):
        tile = pn[pl.ds(j, 128, stride=8), :].astype(BF)
        bt[pl.ds(j, 8, stride=8), :] = nt(bwt, tile)
    bg[zl, x, rj] = bt[...].astype(BF)

    for k, w in enumerate((wq, wk, wv, wg)):
        wbuf[rj, pl.ds(k * 64, 64), :] = w[...]
    wbuf[rj, pl.ds(256, 64), :] = wo[...]

    pl.semaphore_wait(barrier, 19 - 2 * diagonal.astype(jnp.int32))

    for d in (1, 2, 3):
        rcopy(bg.at[zl, x, rj], bg.at[zl, x, rj], BZ + d - 1, zpeer[d - 1]).start()

    xcopy.wait()

    def norm_x(s, carry):
        xn[s, ri] = norm(xin[s].astype(F32), fscale[...]).astype(BF)
        rcopy(xn.at[s, ri], xn.at[s, ri], XZ + s, {"ri": opp}).start()
        rcopy(xn.at[s, ri], xn.at[s, ri], XM + s, {"ri": mate}).start()
        return carry

    lax.fori_loop(0, 4, norm_x, 0)
    for d in (1, 2, 3):
        rcopy(wbuf.at[rj], wbuf.at[rj], WT + d - 1, ypeer[d - 1]).start()

    for d in (1, 2, 3):
        arrived(bg.at[behind(zl, d), x, rj], BZ + d - 1)
    for d in (1, 2, 3):
        rcopy(bg.at[:, x, rj], bg.at[:, x, rj], BY + d - 1, ypeer[d - 1]).start()

    row128 = lax.broadcasted_iota(jnp.int32, (128, 128), 0)
    col128 = lax.broadcasted_iota(jnp.int32, (128, 128), 1)
    ones = jnp.ones((128, 128), BF)
    for b in range(4):
        res = resm[pl.ds(b, 1), :].astype(F32)
        spread = jnp.where(row128 == col128, jnp.broadcast_to(res, (128, 128)), 0.0).astype(BF)
        cm[b] = mm(spread, ones)
    for b in range(2):
        gbt[pl.ds(b * 128, 128), :] = jnp.transpose(
            jnp.broadcast_to(gb[:, pl.ds(b * 128, 128)], (128, 128))
        )
    e128 = eye(128)
    for k in range(4):
        wst[pl.ds(k * 128, 128), :] = nt(e128, ow[pl.ds(k * 256, 256), :]).astype(BF)
    pick = (
        lax.broadcasted_iota(jnp.int32, (32, 128), 0)
        == lax.rem(lax.broadcasted_iota(jnp.int32, (32, 128), 1), 32)
    ).astype(F32).astype(BF)
    p1t = p1[...]
    p2r = jnp.concatenate([p2[...]] * 4, 0)
    total = jnp.maximum(jnp.sum(rowv[...].astype(F32)), 1.0)

    for d in (1, 2, 3):
        arrived(bg.at[:, x, behind(rj, d)], BY + d - 1)
    for d in (1, 2, 3):
        rcopy(bg.at[:, x], bg.at[:, x], BX + d - 1, xpeer[d - 1]).start()

    def forward(s):
        arrived(xn.at[s, opp], XZ + s)
        rcopy(xn.at[s, opp], xn.at[s, opp], XF + s, {"ri": mate}).start()

    forward(0)
    for d in (1, 2, 3):
        arrived(wbuf.at[behind(rj, d)], WT + d - 1)
    for d in (1, 2, 3):
        arrived(bg.at[:, behind(x, d)], BX + d - 1)

    keymask = (jnp.concatenate([cm[b] for b in range(4)], 0) - 1.0) * 1e9
    for hp in range(4):
        two = bg[:, :, :, pl.ds(hp * 16, 16), :].astype(F32).reshape(64, 2, 8, 128)
        for h in range(2):
            biasf[hp * 2 + h] = two[:, h].reshape(512, 128) + keymask

    def weight(k):
        return wbuf[:, pl.ds(k * 64, 64), :].reshape(256, 256)

    lane8 = lax.div(lax.broadcasted_iota(jnp.int32, (8, 128), 1), 32)

    def attend(s, carry):
        @pl.when(s < 3)
        def _():
            forward(s + 1)

        arrived(xn.at[s, mate], XM + s)
        arrived(xn.at[s, oppmate], XF + s)
        every = xn[s].reshape(512, 256)
        own = xn[s, ri]
        key = nt(every, weight(1)).astype(BF)
        value = nt(weight(2), every).astype(BF)
        query = (nt(weight(0), own) * 32 ** -0.5).astype(BF)
        gate = jax.nn.sigmoid(nt(weight(3), own) + gbt[...])
        parts = []
        for h in range(8):
            g, r = h // 4, h % 4
            pieces = [jnp.zeros((32, 128), BF)] * 4
            pieces[r] = query[h * 32 : h * 32 + 32]
            logits = mm(key[:, g * 128 : g * 128 + 128], jnp.concatenate(pieces, 0)) + biasf[h]
            top = jnp.max(logits, 0, keepdims=True)
            probs = jnp.exp(logits - top)
            denom = jnp.sum(probs, 0, keepdims=True)
            head = mm(value[h * 32 : h * 32 + 32], probs.astype(BF))
            parts.append(head * (1.0 / denom))
        attended = (jnp.concatenate(parts, 0) * gate).astype(BF)
        attended = nt(e128, attended).astype(BF)
        result = (xin[s].astype(F32) + mm(attended, weight(4))).astype(BF)
        al[s] = result
        pltpu.make_async_copy(al.at[s], out_al.at[rj * 4 + s], osem.at[s]).start()
        for d in (1, 2, 3):
            rcopy(al.at[s], out_al.at[rj * 4 + s], AL + s * 3 + d - 1, ypeer[d - 1]).start()
        on = norm(result.astype(F32), cscale[...])
        keep = cm[ri] * rows[seq * 16 + rj * 4 + s].astype(F32)
        on = (on * jnp.concatenate([keep, keep], 1)).astype(BF)
        left = nt(p1t, on)
        right = nt(on, p2r)
        for y in range(4):
            ltile = jnp.zeros((8, 128), F32)
            rtile = jnp.zeros((8, 128), F32)
            for k in range(4):
                piece = left[k * 8 : k * 8 + 8]
                if k != y:
                    piece = pltpu.roll(piece, (32 * (k - y)) % 128, 1)
                ltile = jnp.where(lane8 == k, piece, ltile)
                rtile = jnp.where(lane8 == k, right[y * 32 + k * 8 : y * 32 + k * 8 + 8], rtile)
            sndf[y, pl.ds(pl.multiple_of(s * 8, 8), 8), :] = ltile
            sndf[y, pl.ds(pl.multiple_of(32 + s * 8, 8), 8), :] = rtile
        return carry

    lax.fori_loop(0, 4, attend, 0)

    snd[...] = sndf[...].astype(BF)
    for d in (1, 2, 3):
        rcopy(snd.at[ahead(rj, d)], rcv.at[rj], A2 + d - 1, ypeer[d - 1]).start()
    rcv[rj] = snd[rj]
    for d in (1, 2, 3):
        arrived(rcv.at[behind(rj, d)], A2 + d - 1)
    for y in range(4):
        block = rcv[y].astype(F32)
        for side in range(2):
            for s in range(4):
                r = side * 32 + s * 8
                scr[side, pl.ds(y * 4 + s, 8, stride=16), :] = block[r : r + 8]
    lb[:, pl.ds(seq, 1)] = scr[0].astype(BF).reshape(8, 1, 16, 128)
    rblock = scr[1].astype(BF).reshape(8, 16, 128)
    rst[...] = rblock

    @pl.when(diagonal)
    def _():
        rb[:, pl.ds(seq, 1)] = rblock.reshape(8, 1, 16, 128)

    for d in (1, 2, 3):
        rcopy(lb.at[:, seq], lb.at[:, seq], LZ + d - 1, zpeer[d - 1]).start()

    def rfirst(t):
        return rcopy(rst, rb.at[:, seq], R2 + zl, rdest[t], R2 + t)

    for t in range(4):

        @pl.when(jnp.logical_not(jnp.logical_and(diagonal, ri == t)))
        def _():
            rfirst(t).start()

    for b in range(4):
        src = behind(zl, b) * 4 + x
        if b > 0:
            arrived(lb.at[:, src], LZ + b - 1)
        for d in (1, 2, 3):
            rcopy(lb.at[:, src], lb.at[:, src], LX + b * 3 + d - 1, xpeer[d - 1]).start()
        came = b * 4 + rj

        @pl.when(jnp.logical_not(jnp.logical_and(diagonal, zl == b)))
        def _():
            arrived(rb.at[:, came], R2 + b)

        for d in (1, 2, 3):
            rcopy(rb.at[:, came], rb.at[:, came], R4 + b * 3 + d - 1, ypeer[d - 1]).start()

    for b in range(4):
        for d in (1, 2, 3):
            arrived(lb.at[:, behind(zl, b) * 4 + behind(x, d)], LX + b * 3 + d - 1)
            arrived(rb.at[:, b * 4 + behind(rj, d)], R4 + b * 3 + d - 1)

    lane128 = lax.div(lax.broadcasted_iota(jnp.int32, (128, 128), 1), 32)

    def product(q, carry):
        right = nt(e128, rb[q].reshape(256, 128)).astype(BF)
        for k in range(8):
            outer = mm(right, lb[k].reshape(256, 128)).astype(BF)
            for j in range(4):
                bscr[j // 2, pl.ds(k * 32, 32), pl.ds((j % 2) * 128, 128)] = outer[
                    j * 32 : j * 32 + 32
                ]
        for jp in range(2):
            wide = mm(wst[...], bscr[jp])
            for half in range(2):
                c = half * 128
                mixed = wide[0:128, c : c + 128]
                for k in range(1, 4):
                    mixed = jnp.where(
                        lane128 == k, wide[k * 128 : k * 128 + 128, c : c + 128], mixed
                    )
                ub[jp * 2 + half, pl.ds(q, 32, stride=8), :] = nt(pick, mixed.astype(BF))
        return carry

    lax.fori_loop(0, 8, product, 0)
    ubf[...] = ub[...].astype(BF)
    for d in (1, 2, 3):
        rcopy(ubf.at[ahead(rj, d)], urecv.at[rj], UP + d - 1, ypeer[d - 1]).start()
    urecv[rj] = ubf[rj]
    scale = 1.0 / total
    for d in (1, 2, 3):
        arrived(urecv.at[behind(rj, d)], UP + d - 1)
    out_pair[...] = (
        pair[...].astype(F32) + urecv[...].reshape(1024, 128).astype(F32) * scale
    ).astype(BF)

    for s in range(4):
        pltpu.make_async_copy(al.at[s], out_al.at[rj * 4 + s], osem.at[s]).wait()
        left_here(xn.at[s, ri], XZ + s)
        left_here(xn.at[s, ri], XM + s)
        left_here(xn.at[s, opp], XF + s)
        for d in (1, 2, 3):
            left_here(al.at[s], AL + s * 3 + d - 1)
            arrived(out_al.at[behind(rj, d) * 4 + s], AL + s * 3 + d - 1)
    for d in (1, 2, 3):
        left_here(wbuf.at[rj], WT + d - 1)
        left_here(bg.at[zl, x, rj], BZ + d - 1)
        left_here(bg.at[:, x, rj], BY + d - 1)
        left_here(bg.at[:, x], BX + d - 1)
        left_here(snd.at[ahead(rj, d)], A2 + d - 1)
        left_here(lb.at[:, seq], LZ + d - 1)
        left_here(ubf.at[ahead(rj, d)], UP + d - 1)
        for b in range(4):
            left_here(lb.at[:, behind(zl, b) * 4 + x], LX + b * 3 + d - 1)
            left_here(rb.at[:, b * 4 + rj], R4 + b * 3 + d - 1)
    for t in range(4):

        @pl.when(jnp.logical_not(jnp.logical_and(diagonal, ri == t)))
        def _():
            left_here(rst, R2 + t)


def on_device(
    homolog_embedding,
    pairwise_state,
    residue_mask,
    alignment_row_mask,
    focus_layer_scale,
    asking_projector,
    lookup_projector,
    content_projector,
    sigmoid_projector,
    gate_offset_bias,
    final_projector,
    pairwise_norm_gain,
    bias_weight,
    cross_layer_scale,
    first_cross_projector,
    second_cross_projector,
    outer_weight,
):
    vmem = pl.BlockSpec(memory_space=pltpu.VMEM)
    smem = pl.BlockSpec(memory_space=pltpu.SMEM)
    hbm = pl.BlockSpec(memory_space=pl.ANY)
    alignment_output, pair_rows = pl.pallas_call(
        kernel,
        out_shape=(
            jax.ShapeDtypeStruct((16, 128, 256), BF),
            jax.ShapeDtypeStruct((1024, 128), BF),
        ),
        in_specs=[hbm, vmem, vmem, smem] + [vmem] * 14,
        out_specs=(hbm, vmem),
        scratch_shapes=[
            pltpu.VMEM((4, 128, 256), BF),
            pltpu.VMEM((4, 4, 128, 256), BF),
            pltpu.VMEM((4, 320, 256), BF),
            pltpu.VMEM((1024, 128), F32),
            pltpu.VMEM((64, 128), F32),
            pltpu.VMEM((4, 4, 4, 64, 128), BF),
            pltpu.VMEM((8, 512, 128), F32),
            pltpu.VMEM((256, 128), F32),
            pltpu.VMEM((4, 128, 128), F32),
            pltpu.VMEM((512, 256), BF),
            pltpu.VMEM((4, 128, 256), BF),
            pltpu.VMEM((4, 64, 128), F32),
            pltpu.VMEM((4, 64, 128), BF),
            pltpu.VMEM((4, 64, 128), BF),
            pltpu.VMEM((2, 128, 128), F32),
            pltpu.VMEM((8, 16, 16, 128), BF),
            pltpu.VMEM((8, 16, 128), BF),
            pltpu.VMEM((8, 16, 16, 128), BF),
            pltpu.VMEM((2, 256, 256), BF),
            pltpu.VMEM((4, 256, 128), F32),
            pltpu.VMEM((4, 256, 128), BF),
            pltpu.VMEM((4, 256, 128), BF),
            pltpu.SemaphoreType.DMA((COUNT,)),
            pltpu.SemaphoreType.DMA((COUNT,)),
            pltpu.SemaphoreType.DMA,
            pltpu.SemaphoreType.DMA((4,)),
        ],
        compiler_params=pltpu.CompilerParams(
            collective_id=0, has_side_effects=True, vmem_limit_bytes=40 * 1024 * 1024
        ),
        cost_estimate=pl.CostEstimate(
            flops=4_000_000_000, bytes_accessed=4_000_000, transcendentals=2_000_000
        ),
    )(
        homolog_embedding,
        pairwise_state.reshape(1024, 128),
        residue_mask.reshape(4, 128),
        alignment_row_mask,
        alignment_row_mask.reshape(2, 128),
        focus_layer_scale.reshape(1, 256),
        asking_projector.T,
        lookup_projector.T,
        content_projector.T,
        sigmoid_projector.T,
        gate_offset_bias.reshape(1, 256),
        final_projector,
        pairwise_norm_gain.reshape(1, 128),
        bias_weight.T,
        cross_layer_scale.reshape(1, 256),
        first_cross_projector.T,
        second_cross_projector.T,
        outer_weight,
    )
    return alignment_output, pair_rows.reshape(128, 8, 128)


def solution(mesh):
    placed = (
        P("seq", "ri", None),
        P("ri", ("seq", "rj"), None),
        P(),
        P(),
        P(),
        P(None, "rj"),
        P(None, "rj"),
        P(None, "rj"),
        P(None, "rj"),
        P(),
        P("rj", None),
        P(),
        P(),
        P(),
        P(),
        P(),
        P(),
    )
    return jax.shard_map(
        on_device,
        mesh=mesh,
        in_specs=placed,
        out_specs=(P("seq", "ri", None), P("ri", ("seq", "rj"), None)),
        check_vma=False,
    )
```

time: 791 us -> 105 us (0.13)
  waiting for transfers between devices: 561 us -> 0 us
  matrix products: 143 us -> 0 us
  Pallas kernels: 0 us -> 93.8 us
  local copies, waits for them, and re-layouts: 44.8 us -> 10 us
  between operations: 14.2 us -> 0.72 us
  other arithmetic: 12.7 us -> 0 us
  blocking collectives: 11.7 us -> 0 us
    all_gather x3 -> x0, waiting for transfers between devices: 396 us -> none  [the longest x1 342 us: on_device(): bias_full = lax.all_gather(bias_tile, ('seq', 'rj'), axis=2, tiled=True)]
    dot_general x41 -> x0, matrix products: 143 us -> none  [the longest x16 109 us: one_group(): return jnp.einsum('cikl,klz->ciz', outer_part, w_cube, precision=highest)]
    reduce_scatter x1 -> x0, waiting for transfers between devices: 108 us -> none  [on_device(): lax.psum_scatter(lax.map(one_group, grouped).reshape(amount, residue_bloc...]
    pallas_call x0 -> x1, Pallas kernels: none -> 93.8 us  [on_device(): pl.pallas_call(kernel, out_shape=(jax.ShapeDtypeStruct((16, 128, 256), BF...]
    psum x1 -> x0, waiting for transfers between devices: 56.7 us -> none  [on_device(): summed_output = lax.psum(partial_out, 'rj')]
    dynamic_update_slice x16 -> x0, local copies, waits for them, and re-layouts: 18.6 us -> none  [on_device(): lax.map(one_group, grouped).reshape(amount, residue_block, pair_width)]
    dynamic_slice x21 -> x0, local copies, waits for them, and re-layouts: 14 us -> none  [the longest x16 12.2 us: on_device(): lax.map(one_group, grouped).reshape(amount, residue_block, pair_width)]
    all_gather x1 -> x0, blocking collectives: 11.7 us -> none  [on_device(): right_every_res = lax.all_gather(right, 'ri', axis=2, tiled=True)]
  transfers between devices with their start and end apart: 5 -> 0, of which waited for: 5 -> 0; matrix products, arithmetic and copies ran while one was open for 2% -> 0% of each run, Pallas kernels for 0% -> 0%
where the time goes in v1:
time: 105 us
  Pallas kernels  93.8 us (89%)
  local copies, waits for them, and re-layouts  10 us (10%)
    pallas_call x1, Pallas kernels, on_device(): pl.pallas_call(kernel, out_shape=(jax.ShapeDtypeStruct((16, 128, 256), BF...  93.8 us
    unnamed x36, local copies, waits for them, and re-layouts  10 us

profile of v1, /device:TPU:16, one launch (start us, length us, event | category | flops | bytes accessed | tf_op | source)
XLA Modules:
  0.0 104.5 jit_solution(1902440267331792751)
XLA Ops:
  0.6 0.0 copy-start.8
  0.6 0.0 copy-start.15
  0.7 0.0 copy-start.13
  0.7 0.0 copy-start.14
  0.7 0.0 copy-start.11
  0.7 0.0 copy-start.10
  0.7 0.0 copy-start.12
  0.7 0.6 copy-done.8
  1.4 0.0 copy-done.14
  1.4 0.0 copy-done.11
  1.4 0.0 copy-done.10
  1.4 0.0 copy-done.12
  1.4 1.2 %copy-done = bf16[16,128,256]{2,1,0:T(8,128)(2,1)S(1)} copy-done((bf16[16,128,256]{2,1,0:T(8,128)(2,1)S(1)}, bf16[16,128,256]{2,1,0:T(8,128)(2,1)}, u32[]{:S(2)}) %copy-start) | copy-done | bytes 1048600
  2.6 0.9 copy-done.1
  3.6 0.9 copy-done.2
  4.5 0.8 copy-done.3
  5.3 0.8 copy-done.4
  6.1 0.8 copy-done.5
  6.8 0.8 copy-done.6
  7.6 0.8 copy-done.7
  8.3 0.7 copy-done.9
  9.1 93.8 %shard_map.176 = (bf16[16,128,256]{2,1,0:T(8,128)(2,1)S(1)}, bf16[1024,128]{1,0:T(8,128)(2,1)S(1)}) custom-call(bf16[16,128,256]{2,1,0:T(8,128)(2,1)S(1)} %copy-done, bf16[1024,128]{1,0:T(8,128)(2,1)S(1)} %bitcast.16, s32[4,128]{1,0:T(4,128)S(1)} %bitcast.23, s32[256]{0:T(256)S(1)} %copy-done.12, s32[2,128]{1,0:T(2,128)S(1)} %bitcast.25, ...), custom_call_target="tpu_custom_call" | custom-call | flops 4000000000 | bytes 4000000 | tf_op jit(solution)/shard_map/pallas_call | solution.py:371
  102.8 1.0 copy.21
  103.8 0.7 copy.22
  (13 shorter events, 0.0 us)
Async XLA Ops:
  0.6 0.7 copy-start.8
  0.6 0.7 copy-start.15
  0.7 0.7 copy-start.13
  0.7 0.7 copy-start.14
  0.7 0.7 copy-start.11
  0.7 0.7 copy-start.10
  0.7 0.7 copy-start.12
  0.7 0.7 copy-start.16
  1.4 1.2 %copy-start = (bf16[16,128,256]{2,1,0:T(8,128)(2,1)S(1)}, bf16[16,128,256]{2,1,0:T(8,128)(2,1)}, u32[]{:S(2)}) copy-start(bf16[16,128,256]{2,1,0:T(8,128)(2,1)} %hom.1) | copy-start | bytes 3145732
  2.6 0.9 copy-start.1
  3.6 0.9 copy-start.2
  4.5 0.8 copy-start.3
  5.3 0.8 copy-start.4
  6.1 0.8 copy-start.5
  6.8 0.8 copy-start.6
  7.6 0.8 copy-start.7
  8.3 0.7 copy-start.9

commit v2 on v1

--- a/solution.py
+++ b/solution.py
@@ -10,12 +10,12 @@
 NT = (((1,), (1,)), ((), ()))
 
 XZ, XM, XF = 0, 4, 8
-WT, BZ, BY, BX = 12, 15, 18, 21
-AL, A2 = 24, 36
-LZ, LX = 39, 42
-R2, R4 = 54, 58
-UP = 70
-COUNT = 73
+WT, BZ, BY, BX = 12, 16, 19, 23
+AL, A2 = 27, 43
+LZ, LX = 46, 49
+R2, R4 = 65, 69
+UP = 85
+COUNT = 88
 
 
 def nt(a, b):
@@ -39,11 +39,13 @@
 
 
 def kernel(
-    hom, pair, resm, rows, rowv, fscale, wq, wk, wv, wg, gb, wo, pgain, bw, cscale, p1, p2, ow,
+    hom, pair_in, resm_in, rows_in, rowv_in, fscale_in, wq, wk, wv, wg, gb_in, wo, pgain_in, bw_in,
+    cscale_in, p1_in, p2_in, ow_in,
     out_al, out_pair,
-    xin, xn, wbuf, pn, bt, bg, biasf, gbt, cm, wst, al, sndf, snd, rcv, scr, lb, rst, rb,
+    xin, pair, resm, rows, rowv, fscale, gb, pgain, bw, cscale, p1, p2, ow,
+    xn, wbuf, pn, bt, bg, biasf, gbt, cm, wst, al, sndf, snd, rcv, scr, lb, rst, rb,
     bscr, ub, ubf, urecv,
-    ssem, rsem, xsem, osem,
+    ssem, rsem, lsem, osem,
 ):
     seq = lax.axis_index("seq")
     ri = lax.axis_index("ri")
@@ -59,6 +61,8 @@
     def behind(v, d):
         return lax.rem(v + 4 - d, 4)
 
+    plus_y, minus_y = {"rj": ahead(rj, 1)}, {"rj": behind(rj, 1)}
+    plus_x, minus_x = {"seq": zl * 4 + ahead(x, 1)}, {"seq": zl * 4 + behind(x, 1)}
     ypeer = [{"rj": ahead(rj, d)} for d in (1, 2, 3)]
     xpeer = [{"seq": zl * 4 + ahead(x, d)} for d in (1, 2, 3)]
     zpeer = [{"seq": ahead(zl, d) * 4 + x} for d in (1, 2, 3)]
@@ -82,6 +86,59 @@
     def left_here(ref, k):
         pltpu.make_async_copy(ref, ref, ssem.at[k]).wait()
 
+    def ring_start(own, k, plus, minus):
+        rcopy(own, own, k, plus).start()
+        rcopy(own, own, k + 1, minus).start()
+
+    def ring_pass(before, after, lower, upper, k, plus, minus):
+        arrived(before, k)
+        rcopy(lower(before), lower(before), k + 2, plus).start()
+        arrived(after, k + 1)
+        rcopy(upper(after), upper(after), k + 3, minus).start()
+
+    def ring_end(far, lower, upper, k):
+        arrived(lower(far), k + 2)
+        arrived(upper(far), k + 3)
+
+    def ring_sent(own, lower, upper, k):
+        left_here(own, k)
+        left_here(own, k + 1)
+        left_here(lower(own), k + 2)
+        left_here(upper(own), k + 3)
+
+    def first(n):
+        return lambda ref: ref.at[pl.ds(0, n)]
+
+    def second(n):
+        return lambda ref: ref.at[pl.ds(n, n)]
+
+    inward = [
+        (hom.at[pl.ds(rj * 4, 4)], xin),
+        (fscale_in, fscale),
+        (pair_in, pair),
+        (pgain_in, pgain),
+        (bw_in, bw),
+        (wq, wbuf.at[rj, pl.ds(0, 64)]),
+        (wk, wbuf.at[rj, pl.ds(64, 64)]),
+        (wv, wbuf.at[rj, pl.ds(128, 64)]),
+        (wg, wbuf.at[rj, pl.ds(192, 64)]),
+        (wo, wbuf.at[rj, pl.ds(256, 64)]),
+        (resm_in, resm),
+        (rows_in, rows),
+        (rowv_in, rowv),
+        (gb_in, gb),
+        (cscale_in, cscale),
+        (p1_in, p1),
+        (p2_in, p2),
+        (ow_in, ow),
+    ]
+
+    def local(k):
+        return pltpu.make_async_copy(inward[k][0], inward[k][1], lsem.at[k])
+
+    for k in range(len(inward)):
+        local(k).start()
+
     barrier = pltpu.get_barrier_semaphore()
 
     def greet(dev):
@@ -99,41 +156,48 @@
         def _():
             greet(rsrc[t])
 
-    xcopy = pltpu.make_async_copy(hom.at[pl.ds(rj * 4, 4)], xin, xsem)
-    xcopy.start()
-
+    local(0).wait()
+    local(1).wait()
+
+    def norm_x(s, carry):
+        xn[s, ri] = norm(xin[s].astype(F32), fscale[...]).astype(BF)
+        return carry
+
+    lax.fori_loop(0, 4, norm_x, 0)
+
+    pl.semaphore_wait(barrier, 19 - 2 * diagonal.astype(jnp.int32))
+
+    def send_x(s):
+        rcopy(xn.at[s, ri], xn.at[s, ri], XZ + s, {"ri": opp}).start()
+        rcopy(xn.at[s, ri], xn.at[s, ri], XM + s, {"ri": mate}).start()
+
+    send_x(0)
+    for k in range(5, 10):
+        local(k).wait()
+    w_lower, w_upper = first(160), second(160)
+    ring_start(wbuf.at[rj], WT, plus_y, minus_y)
+
+    for k in range(2, 5):
+        local(k).wait()
     pn[...] = norm(pair[...].astype(F32), pgain[...]).astype(BF).astype(F32)
-    bwt = bw[...]
     for j in range(8):
         tile = pn[pl.ds(j, 128, stride=8), :].astype(BF)
-        bt[pl.ds(j, 8, stride=8), :] = nt(bwt, tile)
+        bt[pl.ds(j, 8, stride=8), :] = nt(bw[...], tile)
     bg[zl, x, rj] = bt[...].astype(BF)
-
-    for k, w in enumerate((wq, wk, wv, wg)):
-        wbuf[rj, pl.ds(k * 64, 64), :] = w[...]
-    wbuf[rj, pl.ds(256, 64), :] = wo[...]
-
-    pl.semaphore_wait(barrier, 19 - 2 * diagonal.astype(jnp.int32))
-
     for d in (1, 2, 3):
         rcopy(bg.at[zl, x, rj], bg.at[zl, x, rj], BZ + d - 1, zpeer[d - 1]).start()
-
-    xcopy.wait()
-
-    def norm_x(s, carry):
-        xn[s, ri] = norm(xin[s].astype(F32), fscale[...]).astype(BF)
-        rcopy(xn.at[s, ri], xn.at[s, ri], XZ + s, {"ri": opp}).start()
-        rcopy(xn.at[s, ri], xn.at[s, ri], XM + s, {"ri": mate}).start()
-        return carry
-
-    lax.fori_loop(0, 4, norm_x, 0)
-    for d in (1, 2, 3):
-        rcopy(wbuf.at[rj], wbuf.at[rj], WT + d - 1, ypeer[d - 1]).start()
-
+    for s in range(1, 4):
+        send_x(s)
+
+    for k in range(10, len(inward)):
+        local(k).wait()
+    ring_pass(
+        wbuf.at[behind(rj, 1)], wbuf.at[ahead(rj, 1)], w_lower, w_upper, WT, plus_y, minus_y
+    )
     for d in (1, 2, 3):
         arrived(bg.at[behind(zl, d), x, rj], BZ + d - 1)
-    for d in (1, 2, 3):
-        rcopy(bg.at[:, x, rj], bg.at[:, x, rj], BY + d - 1, ypeer[d - 1]).start()
+    b_lower, b_upper = first(2), second(2)
+    ring_start(bg.at[:, x, rj], BY, plus_y, minus_y)
 
     row128 = lax.broadcasted_iota(jnp.int32, (128, 128), 0)
     col128 = lax.broadcasted_iota(jnp.int32, (128, 128), 1)
@@ -157,20 +221,20 @@
     p2r = jnp.concatenate([p2[...]] * 4, 0)
     total = jnp.maximum(jnp.sum(rowv[...].astype(F32)), 1.0)
 
-    for d in (1, 2, 3):
-        arrived(bg.at[:, x, behind(rj, d)], BY + d - 1)
-    for d in (1, 2, 3):
-        rcopy(bg.at[:, x], bg.at[:, x], BX + d - 1, xpeer[d - 1]).start()
+    ring_pass(
+        bg.at[:, x, behind(rj, 1)], bg.at[:, x, ahead(rj, 1)], b_lower, b_upper, BY, plus_y, minus_y
+    )
+    ring_end(bg.at[:, x, ahead(rj, 2)], b_lower, b_upper, BY)
+    ring_start(bg.at[:, x], BX, plus_x, minus_x)
 
     def forward(s):
         arrived(xn.at[s, opp], XZ + s)
         rcopy(xn.at[s, opp], xn.at[s, opp], XF + s, {"ri": mate}).start()
 
+    ring_pass(bg.at[:, behind(x, 1)], bg.at[:, ahead(x, 1)], b_lower, b_upper, BX, plus_x, minus_x)
     forward(0)
-    for d in (1, 2, 3):
-        arrived(wbuf.at[behind(rj, d)], WT + d - 1)
-    for d in (1, 2, 3):
-        arrived(bg.at[:, behind(x, d)], BX + d - 1)
+    ring_end(wbuf.at[ahead(rj, 2)], w_lower, w_upper, WT)
+    ring_end(bg.at[:, ahead(x, 2)], b_lower, b_upper, BX)
 
     keymask = (jnp.concatenate([cm[b] for b in range(4)], 0) - 1.0) * 1e9
     for hp in range(4):
@@ -212,8 +276,8 @@
         result = (xin[s].astype(F32) + mm(attended, weight(4))).astype(BF)
         al[s] = result
         pltpu.make_async_copy(al.at[s], out_al.at[rj * 4 + s], osem.at[s]).start()
-        for d in (1, 2, 3):
-            rcopy(al.at[s], out_al.at[rj * 4 + s], AL + s * 3 + d - 1, ypeer[d - 1]).start()
+        rcopy(al.at[s], out_al.at[rj * 4 + s], AL + s * 4, plus_y).start()
+        rcopy(al.at[s], out_al.at[rj * 4 + s], AL + s * 4 + 1, minus_y).start()
         on = norm(result.astype(F32), cscale[...])
         keep = cm[ri] * rows[seq * 16 + rj * 4 + s].astype(F32)
         on = (on * jnp.concatenate([keep, keep], 1)).astype(BF)
@@ -230,7 +294,25 @@
                 rtile = jnp.where(lane8 == k, right[y * 32 + k * 8 : y * 32 + k * 8 + 8], rtile)
             sndf[y, pl.ds(pl.multiple_of(s * 8, 8), 8), :] = ltile
             sndf[y, pl.ds(pl.multiple_of(32 + s * 8, 8), 8), :] = rtile
+
+        @pl.when(s > 0)
+        def _():
+            pass_out(s - 1)
+
         return carry
+
+    a_lower, a_upper = first(64), second(64)
+
+    def pass_out(s):
+        ring_pass(
+            out_al.at[behind(rj, 1) * 4 + s],
+            out_al.at[ahead(rj, 1) * 4 + s],
+            a_lower,
+            a_upper,
+            AL + s * 4,
+            plus_y,
+            minus_y,
+        )
 
     lax.fori_loop(0, 4, attend, 0)
 
@@ -266,25 +348,33 @@
         def _():
             rfirst(t).start()
 
+    q_lower, q_upper = first(4), second(4)
     for b in range(4):
         src = behind(zl, b) * 4 + x
         if b > 0:
             arrived(lb.at[:, src], LZ + b - 1)
-        for d in (1, 2, 3):
-            rcopy(lb.at[:, src], lb.at[:, src], LX + b * 3 + d - 1, xpeer[d - 1]).start()
+        ring_start(lb.at[:, src], LX + b * 4, plus_x, minus_x)
         came = b * 4 + rj
 
         @pl.when(jnp.logical_not(jnp.logical_and(diagonal, zl == b)))
         def _():
             arrived(rb.at[:, came], R2 + b)
 
-        for d in (1, 2, 3):
-            rcopy(rb.at[:, came], rb.at[:, came], R4 + b * 3 + d - 1, ypeer[d - 1]).start()
-
+        ring_start(rb.at[:, came], R4 + b * 4, plus_y, minus_y)
     for b in range(4):
-        for d in (1, 2, 3):
-            arrived(lb.at[:, behind(zl, b) * 4 + behind(x, d)], LX + b * 3 + d - 1)
-            arrived(rb.at[:, b * 4 + behind(rj, d)], R4 + b * 3 + d - 1)
+        z4 = behind(zl, b) * 4
+        ring_pass(
+            lb.at[:, z4 + behind(x, 1)], lb.at[:, z4 + ahead(x, 1)], q_lower, q_upper,
+            LX + b * 4, plus_x, minus_x,
+        )
+        ring_pass(
+            rb.at[:, b * 4 + behind(rj, 1)], rb.at[:, b * 4 + ahead(rj, 1)], q_lower, q_upper,
+            R4 + b * 4, plus_y, minus_y,
+        )
+    for b in range(4):
+        ring_end(lb.at[:, behind(zl, b) * 4 + ahead(x, 2)], q_lower, q_upper, LX + b * 4)
+        ring_end(rb.at[:, b * 4 + ahead(rj, 2)], q_lower, q_upper, R4 + b * 4)
+    pass_out(3)
 
     lane128 = lax.div(lax.broadcasted_iota(jnp.int32, (128, 128), 1), 32)
 
@@ -325,20 +415,19 @@
         left_here(xn.at[s, ri], XZ + s)
         left_here(xn.at[s, ri], XM + s)
         left_here(xn.at[s, opp], XF + s)
-        for d in (1, 2, 3):
-            left_here(al.at[s], AL + s * 3 + d - 1)
-            arrived(out_al.at[behind(rj, d) * 4 + s], AL + s * 3 + d - 1)
-    for d in (1, 2, 3):
-        left_here(wbuf.at[rj], WT + d - 1)
+        ring_end(out_al.at[ahead(rj, 2) * 4 + s], a_lower, a_upper, AL + s * 4)
+        ring_sent(al.at[s], a_lower, a_upper, AL + s * 4)
+    ring_sent(wbuf.at[rj], w_lower, w_upper, WT)
+    ring_sent(bg.at[:, x, rj], b_lower, b_upper, BY)
+    ring_sent(bg.at[:, x], b_lower, b_upper, BX)
+    for d in (1, 2, 3):
         left_here(bg.at[zl, x, rj], BZ + d - 1)
-        left_here(bg.at[:, x, rj], BY + d - 1)
-        left_here(bg.at[:, x], BX + d - 1)
         left_here(snd.at[ahead(rj, d)], A2 + d - 1)
         left_here(lb.at[:, seq], LZ + d - 1)
         left_here(ubf.at[ahead(rj, d)], UP + d - 1)
-        for b in range(4):
-            left_here(lb.at[:, behind(zl, b) * 4 + x], LX + b * 3 + d - 1)
-            left_here(rb.at[:, b * 4 + rj], R4 + b * 3 + d - 1)
+    for b in range(4):
+        ring_sent(lb.at[:, behind(zl, b) * 4 + x], q_lower, q_upper, LX + b * 4)
+        ring_sent(rb.at[:, b * 4 + rj], q_lower, q_upper, R4 + b * 4)
     for t in range(4):
 
         @pl.when(jnp.logical_not(jnp.logical_and(diagonal, ri == t)))
@@ -366,7 +455,6 @@
     outer_weight,
 ):
     vmem = pl.BlockSpec(memory_space=pltpu.VMEM)
-    smem = pl.BlockSpec(memory_space=pltpu.SMEM)
     hbm = pl.BlockSpec(memory_space=pl.ANY)
     alignment_output, pair_rows = pl.pallas_call(
         kernel,
@@ -374,10 +462,22 @@
             jax.ShapeDtypeStruct((16, 128, 256), BF),
             jax.ShapeDtypeStruct((1024, 128), BF),
         ),
-        in_specs=[hbm, vmem, vmem, smem] + [vmem] * 14,
+        in_specs=[hbm] * 18,
         out_specs=(hbm, vmem),
         scratch_shapes=[
             pltpu.VMEM((4, 128, 256), BF),
+            pltpu.VMEM((1024, 128), BF),
+            pltpu.VMEM((4, 128), jnp.int32),
+            pltpu.SMEM((256,), jnp.int32),
+            pltpu.VMEM((2, 128), jnp.int32),
+            pltpu.VMEM((1, 256), F32),
+            pltpu.VMEM((1, 256), F32),
+            pltpu.VMEM((1, 128), F32),
+            pltpu.VMEM((8, 128), BF),
+            pltpu.VMEM((1, 256), F32),
+            pltpu.VMEM((32, 256), BF),
+            pltpu.VMEM((32, 256), BF),
+            pltpu.VMEM((1024, 128), BF),
             pltpu.VMEM((4, 4, 128, 256), BF),
             pltpu.VMEM((4, 320, 256), BF),
             pltpu.VMEM((1024, 128), F32),
@@ -401,11 +501,11 @@
             pltpu.VMEM((4, 256, 128), BF),
             pltpu.SemaphoreType.DMA((COUNT,)),
             pltpu.SemaphoreType.DMA((COUNT,)),
-            pltpu.SemaphoreType.DMA,
+            pltpu.SemaphoreType.DMA((18,)),
             pltpu.SemaphoreType.DMA((4,)),
         ],
         compiler_params=pltpu.CompilerParams(
-            collective_id=0, has_side_effects=True, vmem_limit_bytes=40 * 1024 * 1024
+            collective_id=0, has_side_effects=True, vmem_limit_bytes=60 * 1024 * 1024
         ),
         cost_estimate=pl.CostEstimate(
             flops=4_000_000_000, bytes_accessed=4_000_000, transcendentals=2_000_000

time: 105 us -> 102 us (0.971)
  local copies, waits for them, and re-layouts: 10 us -> 3.04 us
  Pallas kernels: 93.8 us -> 97.1 us
    unnamed x36 -> x4, local copies, waits for them, and re-layouts: 10 us -> 3.04 us
    pallas_call x1, Pallas kernels: 93.8 us -> 97.1 us  [on_device(): pl.pallas_call(kernel, out_shape=(jax.ShapeDtypeStruct((16, 128, 256), BF...]
where the time goes in v2:
time: 102 us; the launch traced here: 101 us
  Pallas kernels  97.1 us (95%)
  local copies, waits for them, and re-layouts  3.04 us (3%)
    pallas_call x1, Pallas kernels, on_device(): pl.pallas_call(kernel, out_shape=(jax.ShapeDtypeStruct((16, 128, 256), BF...  97.1 us
    unnamed x4, local copies, waits for them, and re-layouts  3.04 us

profile of v2, /device:TPU:16, one launch (start us, length us, event | category | flops | bytes accessed | tf_op | source)
XLA Modules:
  0.0 100.7 jit_solution(3571391080432975783)
XLA Ops:
  0.6 97.1 %shard_map.176 = (bf16[16,128,256]{2,1,0:T(8,128)(2,1)}, bf16[1024,128]{1,0:T(8,128)(2,1)}) custom-call(bf16[16,128,256]{2,1,0:T(8,128)(2,1)} %hom.1, bf16[1024,128]{1,0:T(8,128)(2,1)} %bitcast.16, s32[4,128]{1,0:T(4,128)} %bitcast.23, s32[256]{0:T(256)} %rows_in.1, s32[2,128]{1,0:T(2,128)} %bitcast.25, f32[1,256]{1,0:T(1,128)} %bitcast.26, ...), custom_call_target="tpu_custom_call" | custom-call | flops 4000000000 | bytes 4000000 | tf_op jit(solution)/shard_map/pallas_call | solution.py:459
  97.7 0.0 copy-start
  97.7 2.3 %copy.21 = bf16[16,128,256]{2,1,0:T(8,128)(2,1)} copy(bf16[16,128,256]{2,1,0:T(8,128)(2,1)} %get-tuple-element.8) | data formatting | bytes 2097152
  100.0 0.0 copy-done
  100.0 0.7 copy.22
Async XLA Ops:
  97.7 2.3 %copy-start = (bf16[1024,128]{1,0:T(8,128)(2,1)S(1)}, bf16[1024,128]{1,0:T(8,128)(2,1)}, u32[]{:S(2)}) copy-start(bf16[1024,128]{1,0:T(8,128)(2,1)} %get-tuple-element.5) | copy-start | bytes 786436

commit v3 on v2

--- a/solution.py
+++ b/solution.py
@@ -9,13 +9,14 @@
 BF = jnp.bfloat16
 NT = (((1,), (1,)), ((), ()))
 
-XZ, XM, XF = 0, 4, 8
-WT, BZ, BY, BX = 12, 16, 19, 23
-AL, A2 = 27, 43
-LZ, LX = 46, 49
-R2, R4 = 65, 69
-UP = 85
-COUNT = 88
+RZ, XZ, XM, XF = 0, 8, 16, 20
+WT, BZ = 24, 28
+AY, AX, BX, BY = 31, 35, 39, 43
+AL, A2 = 47, 63
+LZ, LX = 66, 69
+R2, R4 = 85, 89
+UP = 105
+COUNT = 108
 
 
 def nt(a, b):
@@ -43,7 +44,7 @@
     cscale_in, p1_in, p2_in, ow_in,
     out_al, out_pair,
     xin, pair, resm, rows, rowv, fscale, gb, pgain, bw, cscale, p1, p2, ow,
-    xn, wbuf, pn, bt, bg, biasf, gbt, cm, wst, al, sndf, snd, rcv, scr, lb, rst, rb,
+    xn, relay, wbuf, pn, bt, bg, biasf, gbt, cm, wst, al, right, sndf, snd, rcv, scr, lb, rst, rb,
     bscr, ub, ubf, urecv,
     ssem, rsem, lsem, osem,
 ):
@@ -63,8 +64,18 @@
 
     plus_y, minus_y = {"rj": ahead(rj, 1)}, {"rj": behind(rj, 1)}
     plus_x, minus_x = {"seq": zl * 4 + ahead(x, 1)}, {"seq": zl * 4 + behind(x, 1)}
+    core, z = lax.rem(ri, 2), lax.div(ri, 2) * 4 + zl
+
+    def along_z(step):
+        to = lax.rem(z + step, 8)
+        return lax.div(to, 4) * 2 + core, {
+            "seq": lax.rem(to, 4) * 4 + x,
+            "ri": lax.div(to, 4) * 2 + core,
+        }
+
+    ri_up, up = along_z(2)
+    ri_down, down = along_z(6)
     ypeer = [{"rj": ahead(rj, d)} for d in (1, 2, 3)]
-    xpeer = [{"seq": zl * 4 + ahead(x, d)} for d in (1, 2, 3)]
     zpeer = [{"seq": ahead(zl, d) * 4 + x} for d in (1, 2, 3)]
     rdest = [{"seq": ri * 4 + rj, "ri": t, "rj": x} for t in range(4)]
     rsrc = [{"seq": t * 4 + rj, "ri": zl, "rj": x} for t in range(4)]
@@ -144,7 +155,7 @@
     def greet(dev):
         pl.semaphore_signal(barrier, inc=1, device_id=dev, device_id_type=pl.DeviceIdType.MESH)
 
-    for dev in ypeer + xpeer + zpeer + [{"ri": mate}, {"ri": opp}]:
+    for dev in ypeer + [plus_x, minus_x] + zpeer + [{"ri": mate}, up, down]:
         greet(dev)
     for t in range(4):
 
@@ -168,10 +179,18 @@
     pl.semaphore_wait(barrier, 19 - 2 * diagonal.astype(jnp.int32))
 
     def send_x(s):
-        rcopy(xn.at[s, ri], xn.at[s, ri], XZ + s, {"ri": opp}).start()
+        rcopy(xn.at[s, ri, pl.ds(0, 64)], relay.at[0, s], RZ + s * 2, up).start()
+        rcopy(xn.at[s, ri, pl.ds(64, 64)], relay.at[1, s], RZ + s * 2 + 1, down).start()
         rcopy(xn.at[s, ri], xn.at[s, ri], XM + s, {"ri": mate}).start()
 
-    send_x(0)
+    def relay_x(s):
+        arrived(relay.at[0, s], RZ + s * 2)
+        rcopy(relay.at[0, s], xn.at[s, ri_down, pl.ds(0, 64)], XZ + s * 2, up).start()
+        arrived(relay.at[1, s], RZ + s * 2 + 1)
+        rcopy(relay.at[1, s], xn.at[s, ri_up, pl.ds(64, 64)], XZ + s * 2 + 1, down).start()
+
+    for s in range(4):
+        send_x(s)
     for k in range(5, 10):
         local(k).wait()
     w_lower, w_upper = first(160), second(160)
@@ -183,11 +202,12 @@
     for j in range(8):
         tile = pn[pl.ds(j, 128, stride=8), :].astype(BF)
         bt[pl.ds(j, 8, stride=8), :] = nt(bw[...], tile)
-    bg[zl, x, rj] = bt[...].astype(BF)
+    for half in range(2):
+        bg[half, zl, x, rj] = bt[pl.ds(half * 32, 32), :].astype(BF)
     for d in (1, 2, 3):
-        rcopy(bg.at[zl, x, rj], bg.at[zl, x, rj], BZ + d - 1, zpeer[d - 1]).start()
-    for s in range(1, 4):
-        send_x(s)
+        rcopy(bg.at[:, zl, x, rj], bg.at[:, zl, x, rj], BZ + d - 1, zpeer[d - 1]).start()
+    relay_x(0)
+    relay_x(1)
 
     for k in range(10, len(inward)):
         local(k).wait()
@@ -195,9 +215,11 @@
         wbuf.at[behind(rj, 1)], wbuf.at[ahead(rj, 1)], w_lower, w_upper, WT, plus_y, minus_y
     )
     for d in (1, 2, 3):
-        arrived(bg.at[behind(zl, d), x, rj], BZ + d - 1)
+        arrived(bg.at[:, behind(zl, d), x, rj], BZ + d - 1)
     b_lower, b_upper = first(2), second(2)
-    ring_start(bg.at[:, x, rj], BY, plus_y, minus_y)
+    ring_start(bg.at[0, :, x, rj], AY, plus_y, minus_y)
+    ring_start(bg.at[1, :, x, rj], BX, plus_x, minus_x)
+    relay_x(2)
 
     row128 = lax.broadcasted_iota(jnp.int32, (128, 128), 0)
     col128 = lax.broadcasted_iota(jnp.int32, (128, 128), 1)
@@ -222,23 +244,39 @@
     total = jnp.maximum(jnp.sum(rowv[...].astype(F32)), 1.0)
 
     ring_pass(
-        bg.at[:, x, behind(rj, 1)], bg.at[:, x, ahead(rj, 1)], b_lower, b_upper, BY, plus_y, minus_y
-    )
-    ring_end(bg.at[:, x, ahead(rj, 2)], b_lower, b_upper, BY)
-    ring_start(bg.at[:, x], BX, plus_x, minus_x)
+        bg.at[0, :, x, behind(rj, 1)], bg.at[0, :, x, ahead(rj, 1)], b_lower, b_upper,
+        AY, plus_y, minus_y,
+    )
+    ring_pass(
+        bg.at[1, :, behind(x, 1), rj], bg.at[1, :, ahead(x, 1), rj], b_lower, b_upper,
+        BX, plus_x, minus_x,
+    )
+    ring_end(bg.at[0, :, x, ahead(rj, 2)], b_lower, b_upper, AY)
+    ring_start(bg.at[0, :, x], AX, plus_x, minus_x)
+    ring_end(bg.at[1, :, ahead(x, 2), rj], b_lower, b_upper, BX)
+    ring_start(bg.at[1, :, :, rj], BY, plus_y, minus_y)
+    relay_x(3)
 
     def forward(s):
-        arrived(xn.at[s, opp], XZ + s)
+        arrived(xn.at[s, opp, pl.ds(0, 64)], XZ + s * 2)
+        arrived(xn.at[s, opp, pl.ds(64, 64)], XZ + s * 2 + 1)
         rcopy(xn.at[s, opp], xn.at[s, opp], XF + s, {"ri": mate}).start()
 
-    ring_pass(bg.at[:, behind(x, 1)], bg.at[:, ahead(x, 1)], b_lower, b_upper, BX, plus_x, minus_x)
+    ring_pass(
+        bg.at[0, :, behind(x, 1)], bg.at[0, :, ahead(x, 1)], b_lower, b_upper, AX, plus_x, minus_x
+    )
+    ring_pass(
+        bg.at[1, :, :, behind(rj, 1)], bg.at[1, :, :, ahead(rj, 1)], b_lower, b_upper,
+        BY, plus_y, minus_y,
+    )
     forward(0)
     ring_end(wbuf.at[ahead(rj, 2)], w_lower, w_upper, WT)
-    ring_end(bg.at[:, ahead(x, 2)], b_lower, b_upper, BX)
+    ring_end(bg.at[0, :, ahead(x, 2)], b_lower, b_upper, AX)
+    ring_end(bg.at[1, :, :, ahead(rj, 2)], b_lower, b_upper, BY)
 
     keymask = (jnp.concatenate([cm[b] for b in range(4)], 0) - 1.0) * 1e9
     for hp in range(4):
-        two = bg[:, :, :, pl.ds(hp * 16, 16), :].astype(F32).reshape(64, 2, 8, 128)
+        two = bg[hp // 2, :, :, :, pl.ds(hp % 2 * 16, 16), :].astype(F32).reshape(64, 2, 8, 128)
         for h in range(2):
             biasf[hp * 2 + h] = two[:, h].reshape(512, 128) + keymask
 
@@ -282,7 +320,7 @@
         keep = cm[ri] * rows[seq * 16 + rj * 4 + s].astype(F32)
         on = (on * jnp.concatenate([keep, keep], 1)).astype(BF)
         left = nt(p1t, on)
-        right = nt(on, p2r)
+        right[...] = nt(on, p2r)
         for y in range(4):
             ltile = jnp.zeros((8, 128), F32)
             rtile = jnp.zeros((8, 128), F32)
@@ -291,7 +329,7 @@
                 if k != y:
                     piece = pltpu.roll(piece, (32 * (k - y)) % 128, 1)
                 ltile = jnp.where(lane8 == k, piece, ltile)
-                rtile = jnp.where(lane8 == k, right[y * 32 + k * 8 : y * 32 + k * 8 + 8], rtile)
+                rtile = jnp.where(lane8 == k, right[pl.ds(y * 32 + k, 8, stride=4), :], rtile)
             sndf[y, pl.ds(pl.multiple_of(s * 8, 8), 8), :] = ltile
             sndf[y, pl.ds(pl.multiple_of(32 + s * 8, 8), 8), :] = rtile
 
@@ -378,10 +416,10 @@
 
     lane128 = lax.div(lax.broadcasted_iota(jnp.int32, (128, 128), 1), 32)
 
-    def product(q, carry):
-        right = nt(e128, rb[q].reshape(256, 128)).astype(BF)
+    def product(peer, u):
+        turned = nt(e128, rb[peer * 2 + u].reshape(256, 128)).astype(BF)
         for k in range(8):
-            outer = mm(right, lb[k].reshape(256, 128)).astype(BF)
+            outer = mm(turned, lb[k].reshape(256, 128)).astype(BF)
             for j in range(4):
                 bscr[j // 2, pl.ds(k * 32, 32), pl.ds((j % 2) * 128, 128)] = outer[
                     j * 32 : j * 32 + 32
@@ -395,13 +433,17 @@
                     mixed = jnp.where(
                         lane128 == k, wide[k * 128 : k * 128 + 128, c : c + 128], mixed
                     )
-                ub[jp * 2 + half, pl.ds(q, 32, stride=8), :] = nt(pick, mixed.astype(BF))
-        return carry
-
-    lax.fori_loop(0, 8, product, 0)
-    ubf[...] = ub[...].astype(BF)
-    for d in (1, 2, 3):
-        rcopy(ubf.at[ahead(rj, d)], urecv.at[rj], UP + d - 1, ypeer[d - 1]).start()
+                ub[peer, pl.ds(u * 4 + jp * 2 + half, 32, stride=8), :] = nt(
+                    pick, mixed.astype(BF)
+                )
+
+    for d in (1, 2, 3, 4):
+        peer = ahead(rj, d)
+        for u in range(2):
+            product(peer, u)
+        ubf[peer] = ub[peer].astype(BF)
+        if d < 4:
+            rcopy(ubf.at[peer], urecv.at[rj], UP + d - 1, ypeer[d - 1]).start()
     urecv[rj] = ubf[rj]
     scale = 1.0 / total
     for d in (1, 2, 3):
@@ -412,16 +454,20 @@
 
     for s in range(4):
         pltpu.make_async_copy(al.at[s], out_al.at[rj * 4 + s], osem.at[s]).wait()
-        left_here(xn.at[s, ri], XZ + s)
+        for half in range(2):
+            left_here(relay.at[half, s], RZ + s * 2 + half)
+            left_here(relay.at[half, s], XZ + s * 2 + half)
         left_here(xn.at[s, ri], XM + s)
         left_here(xn.at[s, opp], XF + s)
         ring_end(out_al.at[ahead(rj, 2) * 4 + s], a_lower, a_upper, AL + s * 4)
         ring_sent(al.at[s], a_lower, a_upper, AL + s * 4)
     ring_sent(wbuf.at[rj], w_lower, w_upper, WT)
-    ring_sent(bg.at[:, x, rj], b_lower, b_upper, BY)
-    ring_sent(bg.at[:, x], b_lower, b_upper, BX)
+    ring_sent(bg.at[0, :, x, rj], b_lower, b_upper, AY)
+    ring_sent(bg.at[0, :, x], b_lower, b_upper, AX)
+    ring_sent(bg.at[1, :, x, rj], b_lower, b_upper, BX)
+    ring_sent(bg.at[1, :, :, rj], b_lower, b_upper, BY)
     for d in (1, 2, 3):
-        left_here(bg.at[zl, x, rj], BZ + d - 1)
+        left_here(bg.at[:, zl, x, rj], BZ + d - 1)
         left_here(snd.at[ahead(rj, d)], A2 + d - 1)
         left_here(lb.at[:, seq], LZ + d - 1)
         left_here(ubf.at[ahead(rj, d)], UP + d - 1)
@@ -479,15 +525,17 @@
             pltpu.VMEM((32, 256), BF),
             pltpu.VMEM((1024, 128), BF),
             pltpu.VMEM((4, 4, 128, 256), BF),
+            pltpu.VMEM((2, 4, 64, 256), BF),
             pltpu.VMEM((4, 320, 256), BF),
             pltpu.VMEM((1024, 128), F32),
             pltpu.VMEM((64, 128), F32),
-            pltpu.VMEM((4, 4, 4, 64, 128), BF),
+            pltpu.VMEM((2, 4, 4, 4, 32, 128), BF),
             pltpu.VMEM((8, 512, 128), F32),
             pltpu.VMEM((256, 128), F32),
             pltpu.VMEM((4, 128, 128), F32),
             pltpu.VMEM((512, 256), BF),
             pltpu.VMEM((4, 128, 256), BF),
+            pltpu.VMEM((128, 128), F32),
             pltpu.VMEM((4, 64, 128), F32),
             pltpu.VMEM((4, 64, 128), BF),
             pltpu.VMEM((4, 64, 128), BF),

time: 102 us -> 90.8 us (0.89)
  Pallas kernels: 97.1 us -> 85.3 us
    pallas_call x1, Pallas kernels: 97.1 us -> 85.3 us  [on_device(): pl.pallas_call(kernel, out_shape=(jax.ShapeDtypeStruct((16, 128, 256), BF...]
where the time goes in v3:
time: 90.8 us; the launch traced here: 89 us
  Pallas kernels  85.3 us (94%)
  local copies, waits for them, and re-layouts  3.04 us (3%)
    pallas_call x1, Pallas kernels, on_device(): pl.pallas_call(kernel, out_shape=(jax.ShapeDtypeStruct((16, 128, 256), BF...  85.3 us
    unnamed x4, local copies, waits for them, and re-layouts  3.04 us

profile of v3, /device:TPU:16, one launch (start us, length us, event | category | flops | bytes accessed | tf_op | source)
XLA Modules:
  0.0 89.0 jit_solution(395963306551533054)
XLA Ops:
  0.6 85.3 %shard_map.176 = (bf16[16,128,256]{2,1,0:T(8,128)(2,1)}, bf16[1024,128]{1,0:T(8,128)(2,1)}) custom-call(bf16[16,128,256]{2,1,0:T(8,128)(2,1)} %hom.1, bf16[1024,128]{1,0:T(8,128)(2,1)} %bitcast.16, s32[4,128]{1,0:T(4,128)} %bitcast.23, s32[256]{0:T(256)} %rows_in.1, s32[2,128]{1,0:T(2,128)} %bitcast.25, f32[1,256]{1,0:T(1,128)} %bitcast.26, ...), custom_call_target="tpu_custom_call" | custom-call | flops 4000000000 | bytes 4000000 | tf_op jit(solution)/shard_map/pallas_call | solution.py:505
  85.9 0.0 copy-start
  86.0 2.3 %copy.21 = bf16[16,128,256]{2,1,0:T(8,128)(2,1)} copy(bf16[16,128,256]{2,1,0:T(8,128)(2,1)} %get-tuple-element.8) | data formatting | bytes 2097152
  88.3 0.0 copy-done
  88.3 0.7 copy.22
Async XLA Ops:
  85.9 2.3 %copy-start = (bf16[1024,128]{1,0:T(8,128)(2,1)S(1)}, bf16[1024,128]{1,0:T(8,128)(2,1)}, u32[]{:S(2)}) copy-start(bf16[1024,128]{1,0:T(8,128)(2,1)} %get-tuple-element.5) | copy-start | bytes 786436

commit v4 on v3

--- a/solution.py
+++ b/solution.py
@@ -44,7 +44,7 @@
     cscale_in, p1_in, p2_in, ow_in,
     out_al, out_pair,
     xin, pair, resm, rows, rowv, fscale, gb, pgain, bw, cscale, p1, p2, ow,
-    xn, relay, wbuf, pn, bt, bg, biasf, gbt, cm, wst, al, right, sndf, snd, rcv, scr, lb, rst, rb,
+    xn, relay, wbuf, pn, bt, bg, wkn, wqvg, kb, qt, vt, gate, biasb, gbt, cm, wst, al, right, sndf, snd, rcv, scr, lb, rst, rb,
     bscr, ub, ubf, urecv,
     ssem, rsem, lsem, osem,
 ):
@@ -257,20 +257,59 @@
     ring_start(bg.at[1, :, :, rj], BY, plus_y, minus_y)
     relay_x(3)
 
-    def forward(s):
+    ring_end(wbuf.at[ahead(rj, 2)], w_lower, w_upper, WT)
+
+    def weight(k):
+        return wbuf[:, pl.ds(k * 64, 64), :].reshape(256, 256)
+
+    wkn[...] = nt(eye(256), weight(1)).astype(BF)
+    wqvg[0:256] = weight(0)
+    wqvg[256:512] = weight(2)
+    wqvg[512:768] = weight(3)
+
+    def own_rows(s, carry):
+        block = xn[s, ri]
+        kb[s, ri] = mm(block, wkn[...]).astype(BF)
+        three = nt(wqvg[...], block)
+        qt[s] = (three[0:256] * 32 ** -0.5).astype(BF)
+        vt[s, ri] = three[256:512].astype(BF)
+        gate[s] = jax.nn.sigmoid(three[512:768] + gbt[...])
+        return carry
+
+    def other_rows(s, b):
+        block = xn[s, b]
+        kb[s, b] = mm(block, wkn[...]).astype(BF)
+        vt[s, b] = nt(wqvg[256:512], block).astype(BF)
+
+    lax.fori_loop(0, 4, own_rows, 0)
+    ring_pass(
+        bg.at[0, :, behind(x, 1)], bg.at[0, :, ahead(x, 1)], b_lower, b_upper, AX, plus_x, minus_x
+    )
+    ring_pass(
+        bg.at[1, :, :, behind(rj, 1)], bg.at[1, :, :, ahead(rj, 1)], b_lower, b_upper,
+        BY, plus_y, minus_y,
+    )
+
+    def near_rows(s, carry):
+        arrived(xn.at[s, mate], XM + s)
+        other_rows(s, mate)
+        return carry
+
+    def far_rows(s, carry):
         arrived(xn.at[s, opp, pl.ds(0, 64)], XZ + s * 2)
         arrived(xn.at[s, opp, pl.ds(64, 64)], XZ + s * 2 + 1)
         rcopy(xn.at[s, opp], xn.at[s, opp], XF + s, {"ri": mate}).start()
-
-    ring_pass(
-        bg.at[0, :, behind(x, 1)], bg.at[0, :, ahead(x, 1)], b_lower, b_upper, AX, plus_x, minus_x
-    )
-    ring_pass(
-        bg.at[1, :, :, behind(rj, 1)], bg.at[1, :, :, ahead(rj, 1)], b_lower, b_upper,
-        BY, plus_y, minus_y,
-    )
-    forward(0)
-    ring_end(wbuf.at[ahead(rj, 2)], w_lower, w_upper, WT)
+        other_rows(s, opp)
+        return carry
+
+    def last_rows(s, carry):
+        arrived(xn.at[s, oppmate], XF + s)
+        other_rows(s, oppmate)
+        return carry
+
+    lax.fori_loop(0, 4, near_rows, 0)
+    lax.fori_loop(0, 4, far_rows, 0)
+    lax.fori_loop(0, 4, last_rows, 0)
     ring_end(bg.at[0, :, ahead(x, 2)], b_lower, b_upper, AX)
     ring_end(bg.at[1, :, :, ahead(rj, 2)], b_lower, b_upper, BY)
 
@@ -278,44 +317,38 @@
     for hp in range(4):
         two = bg[hp // 2, :, :, :, pl.ds(hp % 2 * 16, 16), :].astype(F32).reshape(64, 2, 8, 128)
         for h in range(2):
-            biasf[hp * 2 + h] = two[:, h].reshape(512, 128) + keymask
-
-    def weight(k):
-        return wbuf[:, pl.ds(k * 64, 64), :].reshape(256, 256)
+            biasb[hp * 2 + h] = (two[:, h].reshape(512, 128) + keymask).astype(BF)
 
     lane8 = lax.div(lax.broadcasted_iota(jnp.int32, (8, 128), 1), 32)
 
     def attend(s, carry):
-        @pl.when(s < 3)
-        def _():
-            forward(s + 1)
-
-        arrived(xn.at[s, mate], XM + s)
-        arrived(xn.at[s, oppmate], XF + s)
-        every = xn[s].reshape(512, 256)
-        own = xn[s, ri]
-        key = nt(every, weight(1)).astype(BF)
-        value = nt(weight(2), every).astype(BF)
-        query = (nt(weight(0), own) * 32 ** -0.5).astype(BF)
-        gate = jax.nn.sigmoid(nt(weight(3), own) + gbt[...])
+        key = kb[s].reshape(512, 256)
+        value = jnp.concatenate([vt[s, b] for b in range(4)], 1)
+        query = qt[s]
         parts = []
         for h in range(8):
             g, r = h // 4, h % 4
-            pieces = [jnp.zeros((32, 128), BF)] * 4
+            pieces = [jnp.zeros((32, 128), BF)] * 4 + [e128]
             pieces[r] = query[h * 32 : h * 32 + 32]
-            logits = mm(key[:, g * 128 : g * 128 + 128], jnp.concatenate(pieces, 0)) + biasf[h]
-            top = jnp.max(logits, 0, keepdims=True)
-            probs = jnp.exp(logits - top)
-            denom = jnp.sum(probs, 0, keepdims=True)
-            head = mm(value[h * 32 : h * 32 + 32], probs.astype(BF))
-            parts.append(head * (1.0 / denom))
-        attended = (jnp.concatenate(parts, 0) * gate).astype(BF)
+            logits = mm(
+                jnp.concatenate([key[:, g * 128 : g * 128 + 128], biasb[h]], 1),
+                jnp.concatenate(pieces, 0),
+            )
+            probs = jnp.exp(logits - jnp.max(logits, 0, keepdims=True)).astype(BF)
+            summed = mm(
+                jnp.concatenate([value[h * 32 : h * 32 + 32], jnp.ones((16, 512), BF)], 0), probs
+            )
+            parts.append(summed[0:32] * (1.0 / summed[32:33]))
+        attended = (jnp.concatenate(parts, 0) * gate[s]).astype(BF)
         attended = nt(e128, attended).astype(BF)
         result = (xin[s].astype(F32) + mm(attended, weight(4))).astype(BF)
         al[s] = result
         pltpu.make_async_copy(al.at[s], out_al.at[rj * 4 + s], osem.at[s]).start()
-        rcopy(al.at[s], out_al.at[rj * 4 + s], AL + s * 4, plus_y).start()
-        rcopy(al.at[s], out_al.at[rj * 4 + s], AL + s * 4 + 1, minus_y).start()
+
+        @pl.when(s < 2)
+        def _():
+            start_out(s)
+
         on = norm(result.astype(F32), cscale[...])
         keep = cm[ri] * rows[seq * 16 + rj * 4 + s].astype(F32)
         on = (on * jnp.concatenate([keep, keep], 1)).astype(BF)
@@ -332,14 +365,13 @@
                 rtile = jnp.where(lane8 == k, right[pl.ds(y * 32 + k, 8, stride=4), :], rtile)
             sndf[y, pl.ds(pl.multiple_of(s * 8, 8), 8), :] = ltile
             sndf[y, pl.ds(pl.multiple_of(32 + s * 8, 8), 8), :] = rtile
-
-        @pl.when(s > 0)
-        def _():
-            pass_out(s - 1)
-
         return carry
 
     a_lower, a_upper = first(64), second(64)
+
+    def start_out(s):
+        rcopy(al.at[s], out_al.at[rj * 4 + s], AL + s * 4, plus_y).start()
+        rcopy(al.at[s], out_al.at[rj * 4 + s], AL + s * 4 + 1, minus_y).start()
 
     def pass_out(s):
         ring_pass(
@@ -386,6 +418,7 @@
         def _():
             rfirst(t).start()
 
+    start_out(2)
     q_lower, q_upper = first(4), second(4)
     for b in range(4):
         src = behind(zl, b) * 4 + x
@@ -412,7 +445,7 @@
     for b in range(4):
         ring_end(lb.at[:, behind(zl, b) * 4 + ahead(x, 2)], q_lower, q_upper, LX + b * 4)
         ring_end(rb.at[:, b * 4 + ahead(rj, 2)], q_lower, q_upper, R4 + b * 4)
-    pass_out(3)
+    start_out(3)
 
     lane128 = lax.div(lax.broadcasted_iota(jnp.int32, (128, 128), 1), 32)
 
@@ -438,6 +471,7 @@
                 )
 
     for d in (1, 2, 3, 4):
+        pass_out(d - 1)
         peer = ahead(rj, d)
         for u in range(2):
             product(peer, u)
@@ -530,7 +564,13 @@
             pltpu.VMEM((1024, 128), F32),
             pltpu.VMEM((64, 128), F32),
             pltpu.VMEM((2, 4, 4, 4, 32, 128), BF),
-            pltpu.VMEM((8, 512, 128), F32),
+            pltpu.VMEM((256, 256), BF),
+            pltpu.VMEM((768, 256), BF),
+            pltpu.VMEM((4, 4, 128, 256), BF),
+            pltpu.VMEM((4, 256, 128), BF),
+            pltpu.VMEM((4, 4, 256, 128), BF),
+            pltpu.VMEM((4, 256, 128), F32),
+            pltpu.VMEM((8, 512, 128), BF),
             pltpu.VMEM((256, 128), F32),
             pltpu.VMEM((4, 128, 128), F32),
             pltpu.VMEM((512, 256), BF),

time: 90.8 us -> 86.4 us (0.952)
  Pallas kernels: 85.3 us -> 81.5 us
    pallas_call x1, Pallas kernels: 85.3 us -> 81.5 us  [on_device(): pl.pallas_call(kernel, out_shape=(jax.ShapeDtypeStruct((16, 128, 256), BF...]
where the time goes in v4:
time: 86.4 us; the launch traced here: 85.2 us
  Pallas kernels  81.5 us (94%)
  local copies, waits for them, and re-layouts  3.04 us (4%)
    pallas_call x1, Pallas kernels, on_device(): pl.pallas_call(kernel, out_shape=(jax.ShapeDtypeStruct((16, 128, 256), BF...  81.5 us
    unnamed x4, local copies, waits for them, and re-layouts  3.04 us

profile of v4, /device:TPU:16, one launch (start us, length us, event | category | flops | bytes accessed | tf_op | source)
XLA Modules:
  0.0 85.2 jit_solution(10087371258836556591)
XLA Ops:
  0.6 81.5 %shard_map.176 = (bf16[16,128,256]{2,1,0:T(8,128)(2,1)}, bf16[1024,128]{1,0:T(8,128)(2,1)}) custom-call(bf16[16,128,256]{2,1,0:T(8,128)(2,1)} %hom.1, bf16[1024,128]{1,0:T(8,128)(2,1)} %bitcast.16, s32[4,128]{1,0:T(4,128)} %bitcast.23, s32[256]{0:T(256)} %rows_in.1, s32[2,128]{1,0:T(2,128)} %bitcast.25, f32[1,256]{1,0:T(1,128)} %bitcast.26, ...), custom_call_target="tpu_custom_call" | custom-call | flops 4000000000 | bytes 4000000 | tf_op jit(solution)/shard_map/pallas_call | solution.py:539
  82.2 0.0 copy-start
  82.2 2.3 %copy.21 = bf16[16,128,256]{2,1,0:T(8,128)(2,1)} copy(bf16[16,128,256]{2,1,0:T(8,128)(2,1)} %get-tuple-element.8) | data formatting | bytes 2097152
  84.5 0.0 copy-done
  84.5 0.7 copy.22
Async XLA Ops:
  82.2 2.3 %copy-start = (bf16[1024,128]{1,0:T(8,128)(2,1)S(1)}, bf16[1024,128]{1,0:T(8,128)(2,1)}, u32[]{:S(2)}) copy-start(bf16[1024,128]{1,0:T(8,128)(2,1)} %get-tuple-element.5) | copy-start | bytes 786436

commit v5 on v4

--- a/solution.py
+++ b/solution.py
@@ -9,14 +9,11 @@
 BF = jnp.bfloat16
 NT = (((1,), (1,)), ((), ()))
 
-RZ, XZ, XM, XF = 0, 8, 16, 20
-WT, BZ = 24, 28
-AY, AX, BX, BY = 31, 35, 39, 43
-AL, A2 = 47, 63
-LZ, LX = 66, 69
-R2, R4 = 85, 89
-UP = 105
-COUNT = 108
+SIZES = (8, 8, 4, 4, 6, 16, 16, 6, 6, 24, 16, 16, 6, 6, 3)
+RZ, XZ, XM, XF, WT, BA, BB, AX, BY, AL, LL, RR, LX, R4, UP = (
+    sum(SIZES[:i]) for i in range(len(SIZES))
+)
+COUNT = sum(SIZES)
 
 
 def nt(a, b):
@@ -44,7 +41,7 @@
     cscale_in, p1_in, p2_in, ow_in,
     out_al, out_pair,
     xin, pair, resm, rows, rowv, fscale, gb, pgain, bw, cscale, p1, p2, ow,
-    xn, relay, wbuf, pn, bt, bg, wkn, wqvg, kb, qt, vt, gate, biasb, gbt, cm, wst, al, right, sndf, snd, rcv, scr, lb, rst, rb,
+    xn, relay, wbuf, pn, bt, bg, wkn, wqvg, kb, qt, vt, gate, biasb, gbt, cm, wst, al, right, sndf, snd, lraw, rraw, scr, lb, rb,
     bscr, ub, ubf, urecv,
     ssem, rsem, lsem, osem,
 ):
@@ -75,11 +72,37 @@
 
     ri_up, up = along_z(2)
     ri_down, down = along_z(6)
-    ypeer = [{"rj": ahead(rj, d)} for d in (1, 2, 3)]
-    zpeer = [{"seq": ahead(zl, d) * 4 + x} for d in (1, 2, 3)]
-    rdest = [{"seq": ri * 4 + rj, "ri": t, "rj": x} for t in range(4)]
-    rsrc = [{"seq": t * 4 + rj, "ri": zl, "rj": x} for t in range(4)]
+
+    def seq_of(zz, xx):
+        return zz * 4 + xx
+
+    def in_zy(n):
+        return {"seq": seq_of(ahead(zl, lax.div(n, 4)), x), "rj": ahead(rj, lax.rem(n, 4))}
+
+    def in_zx(n):
+        return {"seq": seq_of(ahead(zl, lax.div(n, 4)), ahead(x, lax.rem(n, 4)))}
+
+    def right_to(n):
+        return {"seq": seq_of(ri, lax.div(n, 4)), "ri": lax.rem(n, 4), "rj": x}
+
+    def right_from(n):
+        return {"seq": seq_of(lax.div(n, 4), rj), "ri": zl, "rj": lax.rem(n, 4)}
+
+    def each(low, high, body):
+        def step(n, carry):
+            body(n)
+            return carry
+
+        lax.fori_loop(low, high, step, 0)
+
     diagonal = jnp.logical_and(zl == ri, x == rj)
+
+    def to_self(n):
+        return jnp.logical_and(diagonal, n == seq_of(x, ri))
+
+    def from_self(n):
+        return jnp.logical_and(diagonal, n == seq_of(zl, rj))
+
 
     def rcopy(src, dst, k, dev, send=None):
         return pltpu.make_async_remote_copy(
@@ -97,25 +120,27 @@
     def left_here(ref, k):
         pltpu.make_async_copy(ref, ref, ssem.at[k]).wait()
 
-    def ring_start(own, k, plus, minus):
-        rcopy(own, own, k, plus).start()
-        rcopy(own, own, k + 1, minus).start()
+    def ring_start(own, lower, upper, k, plus, minus):
+        for i, (part, dev) in enumerate(
+            ((lower, plus), (upper, minus), (upper, plus), (lower, minus))
+        ):
+            rcopy(part(own), part(own), k + i, dev).start()
 
     def ring_pass(before, after, lower, upper, k, plus, minus):
-        arrived(before, k)
-        rcopy(lower(before), lower(before), k + 2, plus).start()
-        arrived(after, k + 1)
-        rcopy(upper(after), upper(after), k + 3, minus).start()
-
-    def ring_end(far, lower, upper, k):
-        arrived(lower(far), k + 2)
-        arrived(upper(far), k + 3)
+        arrived(lower(before), k)
+        rcopy(lower(before), lower(before), k + 4, plus).start()
+        arrived(upper(after), k + 1)
+        rcopy(upper(after), upper(after), k + 5, minus).start()
+
+    def ring_end(before, after, far, lower, upper, k):
+        arrived(upper(before), k + 2)
+        arrived(lower(after), k + 3)
+        arrived(lower(far), k + 4)
+        arrived(upper(far), k + 5)
 
     def ring_sent(own, lower, upper, k):
-        left_here(own, k)
-        left_here(own, k + 1)
-        left_here(lower(own), k + 2)
-        left_here(upper(own), k + 3)
+        for i, part in enumerate((lower, upper, upper, lower, lower, upper)):
+            left_here(part(own), k + i)
 
     def first(n):
         return lambda ref: ref.at[pl.ds(0, n)]
@@ -155,17 +180,24 @@
     def greet(dev):
         pl.semaphore_signal(barrier, inc=1, device_id=dev, device_id_type=pl.DeviceIdType.MESH)
 
-    for dev in ypeer + [plus_x, minus_x] + zpeer + [{"ri": mate}, up, down]:
+    def greet_all(n):
+        greet(in_zy(n))
+        greet(in_zx(n))
+
+    each(1, 16, greet_all)
+    for dev in ({"ri": mate}, up, down):
         greet(dev)
-    for t in range(4):
-
-        @pl.when(jnp.logical_not(jnp.logical_and(diagonal, ri == t)))
+
+    def greet_right(n):
+        @pl.when(jnp.logical_not(to_self(n)))
         def _():
-            greet(rdest[t])
-
-        @pl.when(jnp.logical_not(jnp.logical_and(diagonal, zl == t)))
+            greet(right_to(n))
+
+        @pl.when(jnp.logical_not(from_self(n)))
         def _():
-            greet(rsrc[t])
+            greet(right_from(n))
+
+    each(0, 16, greet_right)
 
     local(0).wait()
     local(1).wait()
@@ -176,7 +208,7 @@
 
     lax.fori_loop(0, 4, norm_x, 0)
 
-    pl.semaphore_wait(barrier, 19 - 2 * diagonal.astype(jnp.int32))
+    pl.semaphore_wait(barrier, 65 - 2 * diagonal.astype(jnp.int32))
 
     def send_x(s):
         rcopy(xn.at[s, ri, pl.ds(0, 64)], relay.at[0, s], RZ + s * 2, up).start()
@@ -194,7 +226,7 @@
     for k in range(5, 10):
         local(k).wait()
     w_lower, w_upper = first(160), second(160)
-    ring_start(wbuf.at[rj], WT, plus_y, minus_y)
+    ring_start(wbuf.at[rj], w_lower, w_upper, WT, plus_y, minus_y)
 
     for k in range(2, 5):
         local(k).wait()
@@ -204,8 +236,11 @@
         bt[pl.ds(j, 8, stride=8), :] = nt(bw[...], tile)
     for half in range(2):
         bg[half, zl, x, rj] = bt[pl.ds(half * 32, 32), :].astype(BF)
-    for d in (1, 2, 3):
-        rcopy(bg.at[:, zl, x, rj], bg.at[:, zl, x, rj], BZ + d - 1, zpeer[d - 1]).start()
+    def send_bias(n):
+        rcopy(bg.at[0, zl, x, rj], bg.at[0, zl, x, rj], BA + n, in_zy(n)).start()
+        rcopy(bg.at[1, zl, x, rj], bg.at[1, zl, x, rj], BB + n, in_zx(n)).start()
+
+    each(1, 16, send_bias)
     relay_x(0)
     relay_x(1)
 
@@ -214,11 +249,15 @@
     ring_pass(
         wbuf.at[behind(rj, 1)], wbuf.at[ahead(rj, 1)], w_lower, w_upper, WT, plus_y, minus_y
     )
-    for d in (1, 2, 3):
-        arrived(bg.at[:, behind(zl, d), x, rj], BZ + d - 1)
+    def came_bias(n):
+        dz, d = lax.div(n, 4), lax.rem(n, 4)
+        arrived(bg.at[0, behind(zl, dz), x, behind(rj, d)], BA + n)
+        arrived(bg.at[1, behind(zl, dz), behind(x, d), rj], BB + n)
+
+    each(1, 16, came_bias)
     b_lower, b_upper = first(2), second(2)
-    ring_start(bg.at[0, :, x, rj], AY, plus_y, minus_y)
-    ring_start(bg.at[1, :, x, rj], BX, plus_x, minus_x)
+    ring_start(bg.at[0, :, x], b_lower, b_upper, AX, plus_x, minus_x)
+    ring_start(bg.at[1, :, :, rj], b_lower, b_upper, BY, plus_y, minus_y)
     relay_x(2)
 
     row128 = lax.broadcasted_iota(jnp.int32, (128, 128), 0)
@@ -243,21 +282,11 @@
     p2r = jnp.concatenate([p2[...]] * 4, 0)
     total = jnp.maximum(jnp.sum(rowv[...].astype(F32)), 1.0)
 
-    ring_pass(
-        bg.at[0, :, x, behind(rj, 1)], bg.at[0, :, x, ahead(rj, 1)], b_lower, b_upper,
-        AY, plus_y, minus_y,
-    )
-    ring_pass(
-        bg.at[1, :, behind(x, 1), rj], bg.at[1, :, ahead(x, 1), rj], b_lower, b_upper,
-        BX, plus_x, minus_x,
-    )
-    ring_end(bg.at[0, :, x, ahead(rj, 2)], b_lower, b_upper, AY)
-    ring_start(bg.at[0, :, x], AX, plus_x, minus_x)
-    ring_end(bg.at[1, :, ahead(x, 2), rj], b_lower, b_upper, BX)
-    ring_start(bg.at[1, :, :, rj], BY, plus_y, minus_y)
     relay_x(3)
 
-    ring_end(wbuf.at[ahead(rj, 2)], w_lower, w_upper, WT)
+    ring_end(
+        wbuf.at[behind(rj, 1)], wbuf.at[ahead(rj, 1)], wbuf.at[ahead(rj, 2)], w_lower, w_upper, WT
+    )
 
     def weight(k):
         return wbuf[:, pl.ds(k * 64, 64), :].reshape(256, 256)
@@ -310,14 +339,20 @@
     lax.fori_loop(0, 4, near_rows, 0)
     lax.fori_loop(0, 4, far_rows, 0)
     lax.fori_loop(0, 4, last_rows, 0)
-    ring_end(bg.at[0, :, ahead(x, 2)], b_lower, b_upper, AX)
-    ring_end(bg.at[1, :, :, ahead(rj, 2)], b_lower, b_upper, BY)
+    ring_end(
+        bg.at[0, :, behind(x, 1)], bg.at[0, :, ahead(x, 1)], bg.at[0, :, ahead(x, 2)],
+        b_lower, b_upper, AX,
+    )
+    ring_end(
+        bg.at[1, :, :, behind(rj, 1)], bg.at[1, :, :, ahead(rj, 1)], bg.at[1, :, :, ahead(rj, 2)],
+        b_lower, b_upper, BY,
+    )
 
     keymask = (jnp.concatenate([cm[b] for b in range(4)], 0) - 1.0) * 1e9
     for hp in range(4):
         two = bg[hp // 2, :, :, :, pl.ds(hp % 2 * 16, 16), :].astype(F32).reshape(64, 2, 8, 128)
         for h in range(2):
-            biasb[hp * 2 + h] = (two[:, h].reshape(512, 128) + keymask).astype(BF)
+            biasb[hp, :, pl.ds(h * 128, 128)] = (two[:, h].reshape(512, 128) + keymask).astype(F32)
 
     lane8 = lax.div(lax.broadcasted_iota(jnp.int32, (8, 128), 1), 32)
 
@@ -326,19 +361,23 @@
         value = jnp.concatenate([vt[s, b] for b in range(4)], 1)
         query = qt[s]
         parts = []
-        for h in range(8):
-            g, r = h // 4, h % 4
-            pieces = [jnp.zeros((32, 128), BF)] * 4 + [e128]
-            pieces[r] = query[h * 32 : h * 32 + 32]
-            logits = mm(
-                jnp.concatenate([key[:, g * 128 : g * 128 + 128], biasb[h]], 1),
-                jnp.concatenate(pieces, 0),
+        for hp in range(4):
+            g, r = hp // 2, hp % 2 * 2
+            zero = jnp.zeros((32, 128), BF)
+            pair_q = []
+            for h in range(2):
+                pieces = [zero] * 4
+                pieces[r + h] = query[hp * 64 + h * 32 : hp * 64 + h * 32 + 32]
+                pair_q.append(jnp.concatenate(pieces, 0))
+            logits = mm(key[:, g * 128 : g * 128 + 128], jnp.concatenate(pair_q, 1)) + biasb[hp]
+            low = logits - jnp.max(logits, 0, keepdims=True)
+            probs = jnp.exp(low).astype(BF)
+            summed = mm(
+                jnp.concatenate([value[hp * 64 : hp * 64 + 64], jnp.ones((16, 512), BF)], 0), probs
             )
-            probs = jnp.exp(logits - jnp.max(logits, 0, keepdims=True)).astype(BF)
-            summed = mm(
-                jnp.concatenate([value[h * 32 : h * 32 + 32], jnp.ones((16, 512), BF)], 0), probs
-            )
-            parts.append(summed[0:32] * (1.0 / summed[32:33]))
+            scale = 1.0 / summed[64:65]
+            parts.append(summed[0:32, 0:128] * scale[:, 0:128])
+            parts.append(summed[32:64, 128:256] * scale[:, 128:256])
         attended = (jnp.concatenate(parts, 0) * gate[s]).astype(BF)
         attended = nt(e128, attended).astype(BF)
         result = (xin[s].astype(F32) + mm(attended, weight(4))).astype(BF)
@@ -369,87 +408,95 @@
 
     a_lower, a_upper = first(64), second(64)
 
+    def out(s, source):
+        return out_al.at[source * 4 + s]
+
     def start_out(s):
-        rcopy(al.at[s], out_al.at[rj * 4 + s], AL + s * 4, plus_y).start()
-        rcopy(al.at[s], out_al.at[rj * 4 + s], AL + s * 4 + 1, minus_y).start()
+        for i, (part, dev) in enumerate(
+            ((a_lower, plus_y), (a_upper, minus_y), (a_upper, plus_y), (a_lower, minus_y))
+        ):
+            rcopy(part(al.at[s]), part(out(s, rj)), AL + s * 6 + i, dev).start()
 
     def pass_out(s):
         ring_pass(
-            out_al.at[behind(rj, 1) * 4 + s],
-            out_al.at[ahead(rj, 1) * 4 + s],
-            a_lower,
-            a_upper,
-            AL + s * 4,
-            plus_y,
-            minus_y,
+            out(s, behind(rj, 1)), out(s, ahead(rj, 1)), a_lower, a_upper, AL + s * 6,
+            plus_y, minus_y,
         )
 
     lax.fori_loop(0, 4, attend, 0)
 
     snd[...] = sndf[...].astype(BF)
-    for d in (1, 2, 3):
-        rcopy(snd.at[ahead(rj, d)], rcv.at[rj], A2 + d - 1, ypeer[d - 1]).start()
-    rcv[rj] = snd[rj]
-    for d in (1, 2, 3):
-        arrived(rcv.at[behind(rj, d)], A2 + d - 1)
-    for y in range(4):
-        block = rcv[y].astype(F32)
-        for side in range(2):
-            for s in range(4):
-                r = side * 32 + s * 8
-                scr[side, pl.ds(y * 4 + s, 8, stride=16), :] = block[r : r + 8]
-    lb[:, pl.ds(seq, 1)] = scr[0].astype(BF).reshape(8, 1, 16, 128)
-    rblock = scr[1].astype(BF).reshape(8, 16, 128)
-    rst[...] = rblock
+
+    def send_sides(n):
+        rcopy(
+            snd.at[ahead(rj, lax.rem(n, 4)), pl.ds(0, 32)], lraw.at[zl, rj], LL + n, in_zy(n)
+        ).start()
+
+    each(1, 16, send_sides)
+
+    def right_copy(n):
+        return rcopy(
+            snd.at[lax.div(n, 4), pl.ds(32, 32)], rraw.at[zl, rj], RR + zl * 4 + rj, right_to(n),
+            RR + n,
+        )
+
+    def send_right(n):
+        @pl.when(jnp.logical_not(to_self(n)))
+        def _():
+            right_copy(n).start()
+
+    each(0, 16, send_right)
+    start_out(2)
+    start_out(3)
+    lraw[zl, rj] = snd[rj, 0:32]
 
     @pl.when(diagonal)
     def _():
-        rb[:, pl.ds(seq, 1)] = rblock.reshape(8, 1, 16, 128)
-
-    for d in (1, 2, 3):
-        rcopy(lb.at[:, seq], lb.at[:, seq], LZ + d - 1, zpeer[d - 1]).start()
-
-    def rfirst(t):
-        return rcopy(rst, rb.at[:, seq], R2 + zl, rdest[t], R2 + t)
-
-    for t in range(4):
-
-        @pl.when(jnp.logical_not(jnp.logical_and(diagonal, ri == t)))
+        rraw[zl, rj] = snd[x, 32:64]
+
+    def came_left(n):
+        arrived(lraw.at[behind(zl, lax.div(n, 4)), behind(rj, lax.rem(n, 4))], LL + n)
+
+    def came_right(n):
+        @pl.when(jnp.logical_not(from_self(n)))
         def _():
-            rfirst(t).start()
-
-    start_out(2)
+            arrived(rraw.at[lax.div(n, 4), lax.rem(n, 4)], RR + n)
+
+    def regroup(raw, buf, place):
+        def step(t):
+            block = raw[t].astype(F32)
+            for y in range(4):
+                for s in range(4):
+                    scr[pl.ds(y * 4 + s, 8, stride=16), :] = block[y, s * 8 : s * 8 + 8]
+            buf[:, place, t] = scr[...].astype(BF).reshape(8, 16, 128)
+
+        each(0, 4, step)
+
     q_lower, q_upper = first(4), second(4)
-    for b in range(4):
-        src = behind(zl, b) * 4 + x
-        if b > 0:
-            arrived(lb.at[:, src], LZ + b - 1)
-        ring_start(lb.at[:, src], LX + b * 4, plus_x, minus_x)
-        came = b * 4 + rj
-
-        @pl.when(jnp.logical_not(jnp.logical_and(diagonal, zl == b)))
-        def _():
-            arrived(rb.at[:, came], R2 + b)
-
-        ring_start(rb.at[:, came], R4 + b * 4, plus_y, minus_y)
-    for b in range(4):
-        z4 = behind(zl, b) * 4
-        ring_pass(
-            lb.at[:, z4 + behind(x, 1)], lb.at[:, z4 + ahead(x, 1)], q_lower, q_upper,
-            LX + b * 4, plus_x, minus_x,
-        )
-        ring_pass(
-            rb.at[:, b * 4 + behind(rj, 1)], rb.at[:, b * 4 + ahead(rj, 1)], q_lower, q_upper,
-            R4 + b * 4, plus_y, minus_y,
-        )
-    for b in range(4):
-        ring_end(lb.at[:, behind(zl, b) * 4 + ahead(x, 2)], q_lower, q_upper, LX + b * 4)
-        ring_end(rb.at[:, b * 4 + ahead(rj, 2)], q_lower, q_upper, R4 + b * 4)
-    start_out(3)
+    each(1, 16, came_left)
+    regroup(lraw, lb, x)
+    ring_start(lb.at[:, x], q_lower, q_upper, LX, plus_x, minus_x)
+    each(0, 16, came_right)
+    regroup(rraw, rb, rj)
+    ring_start(rb.at[:, rj], q_lower, q_upper, R4, plus_y, minus_y)
+    ring_pass(
+        lb.at[:, behind(x, 1)], lb.at[:, ahead(x, 1)], q_lower, q_upper, LX, plus_x, minus_x
+    )
+    ring_pass(
+        rb.at[:, behind(rj, 1)], rb.at[:, ahead(rj, 1)], q_lower, q_upper, R4, plus_y, minus_y
+    )
+    each(0, 4, pass_out)
+    ring_end(
+        lb.at[:, behind(x, 1)], lb.at[:, ahead(x, 1)], lb.at[:, ahead(x, 2)], q_lower, q_upper, LX
+    )
+    ring_end(
+        rb.at[:, behind(rj, 1)], rb.at[:, ahead(rj, 1)], rb.at[:, ahead(rj, 2)],
+        q_lower, q_upper, R4,
+    )
 
     lane128 = lax.div(lax.broadcasted_iota(jnp.int32, (128, 128), 1), 32)
 
-    def product(peer, u):
+    def product(peer, u, carry):
         turned = nt(e128, rb[peer * 2 + u].reshape(256, 128)).astype(BF)
         for k in range(8):
             outer = mm(turned, lb[k].reshape(256, 128)).astype(BF)
@@ -469,15 +516,22 @@
                 ub[peer, pl.ds(u * 4 + jp * 2 + half, 32, stride=8), :] = nt(
                     pick, mixed.astype(BF)
                 )
-
-    for d in (1, 2, 3, 4):
-        pass_out(d - 1)
+        return carry
+
+    def for_peer(d):
         peer = ahead(rj, d)
-        for u in range(2):
-            product(peer, u)
+        lax.fori_loop(0, 2, lambda u, carry: product(peer, u, carry), 0)
         ubf[peer] = ub[peer].astype(BF)
-        if d < 4:
-            rcopy(ubf.at[peer], urecv.at[rj], UP + d - 1, ypeer[d - 1]).start()
+
+        @pl.when(d < 4)
+        def _():
+            update_copy(d).start()
+
+    def update_copy(d):
+        peer = ahead(rj, d)
+        return rcopy(ubf.at[peer], urecv.at[rj], UP + d - 1, {"rj": peer})
+
+    each(1, 5, for_peer)
     urecv[rj] = ubf[rj]
     scale = 1.0 / total
     for d in (1, 2, 3):
@@ -486,33 +540,40 @@
         pair[...].astype(F32) + urecv[...].reshape(1024, 128).astype(F32) * scale
     ).astype(BF)
 
-    for s in range(4):
+    def drain(s):
         pltpu.make_async_copy(al.at[s], out_al.at[rj * 4 + s], osem.at[s]).wait()
         for half in range(2):
             left_here(relay.at[half, s], RZ + s * 2 + half)
             left_here(relay.at[half, s], XZ + s * 2 + half)
         left_here(xn.at[s, ri], XM + s)
         left_here(xn.at[s, opp], XF + s)
-        ring_end(out_al.at[ahead(rj, 2) * 4 + s], a_lower, a_upper, AL + s * 4)
-        ring_sent(al.at[s], a_lower, a_upper, AL + s * 4)
+        ring_end(
+            out(s, behind(rj, 1)), out(s, ahead(rj, 1)), out(s, ahead(rj, 2)), a_lower, a_upper,
+            AL + s * 6,
+        )
+        ring_sent(al.at[s], a_lower, a_upper, AL + s * 6)
+
+    each(0, 4, drain)
     ring_sent(wbuf.at[rj], w_lower, w_upper, WT)
-    ring_sent(bg.at[0, :, x, rj], b_lower, b_upper, AY)
     ring_sent(bg.at[0, :, x], b_lower, b_upper, AX)
-    ring_sent(bg.at[1, :, x, rj], b_lower, b_upper, BX)
     ring_sent(bg.at[1, :, :, rj], b_lower, b_upper, BY)
-    for d in (1, 2, 3):
-        left_here(bg.at[:, zl, x, rj], BZ + d - 1)
-        left_here(snd.at[ahead(rj, d)], A2 + d - 1)
-        left_here(lb.at[:, seq], LZ + d - 1)
-        left_here(ubf.at[ahead(rj, d)], UP + d - 1)
-    for b in range(4):
-        ring_sent(lb.at[:, behind(zl, b) * 4 + x], q_lower, q_upper, LX + b * 4)
-        ring_sent(rb.at[:, b * 4 + rj], q_lower, q_upper, R4 + b * 4)
-    for t in range(4):
-
-        @pl.when(jnp.logical_not(jnp.logical_and(diagonal, ri == t)))
+    ring_sent(lb.at[:, x], q_lower, q_upper, LX)
+    ring_sent(rb.at[:, rj], q_lower, q_upper, R4)
+
+    def drain_small(n):
+        left_here(bg.at[0, zl, x, rj], BA + n)
+        left_here(bg.at[1, zl, x, rj], BB + n)
+        left_here(lraw.at[zl, rj], LL + n)
+
+    each(1, 16, drain_small)
+
+    def drain_right(n):
+        @pl.when(jnp.logical_not(to_self(n)))
         def _():
-            left_here(rst, R2 + t)
+            left_here(rraw.at[zl, rj], RR + n)
+
+    each(0, 16, drain_right)
+    each(1, 4, lambda d: left_here(ubf.at[ahead(rj, d)], UP + d - 1))
 
 
 def on_device(
@@ -570,7 +631,7 @@
             pltpu.VMEM((4, 256, 128), BF),
             pltpu.VMEM((4, 4, 256, 128), BF),
             pltpu.VMEM((4, 256, 128), F32),
-            pltpu.VMEM((8, 512, 128), BF),
+            pltpu.VMEM((4, 512, 256), F32),
             pltpu.VMEM((256, 128), F32),
             pltpu.VMEM((4, 128, 128), F32),
             pltpu.VMEM((512, 256), BF),
@@ -578,11 +639,11 @@
             pltpu.VMEM((128, 128), F32),
             pltpu.VMEM((4, 64, 128), F32),
             pltpu.VMEM((4, 64, 128), BF),
-            pltpu.VMEM((4, 64, 128), BF),
-            pltpu.VMEM((2, 128, 128), F32),
-            pltpu.VMEM((8, 16, 16, 128), BF),
-            pltpu.VMEM((8, 16, 128), BF),
-            pltpu.VMEM((8, 16, 16, 128), BF),
+            pltpu.VMEM((4, 4, 32, 128), BF),
+            pltpu.VMEM((4, 4, 32, 128), BF),
+            pltpu.VMEM((128, 128), F32),
+            pltpu.VMEM((8, 4, 4, 16, 128), BF),
+            pltpu.VMEM((8, 4, 4, 16, 128), BF),
             pltpu.VMEM((2, 256, 256), BF),
             pltpu.VMEM((4, 256, 128), F32),
             pltpu.VMEM((4, 256, 128), BF),

time: 86.4 us -> 79.6 us (0.921)
  Pallas kernels: 81.5 us -> 75.1 us
    pallas_call x1, Pallas kernels: 81.5 us -> 75.1 us  [on_device(): pl.pallas_call(kernel, out_shape=(jax.ShapeDtypeStruct((16, 128, 256), BF...]
where the time goes in v5:
time: 79.6 us; the launch traced here: 78.8 us
  Pallas kernels  75.1 us (94%)
  local copies, waits for them, and re-layouts  3.04 us (4%)
    pallas_call x1, Pallas kernels, on_device(): pl.pallas_call(kernel, out_shape=(jax.ShapeDtypeStruct((16, 128, 256), BF...  75.1 us
    unnamed x4, local copies, waits for them, and re-layouts  3.04 us

profile of v5, /device:TPU:16, one launch (start us, length us, event | category | flops | bytes accessed | tf_op | source)
XLA Modules:
  0.0 78.8 jit_solution(18406391357289923736)
XLA Ops:
  0.6 75.1 %shard_map.176 = (bf16[16,128,256]{2,1,0:T(8,128)(2,1)}, bf16[1024,128]{1,0:T(8,128)(2,1)}) custom-call(bf16[16,128,256]{2,1,0:T(8,128)(2,1)} %hom.1, bf16[1024,128]{1,0:T(8,128)(2,1)} %bitcast.16, s32[4,128]{1,0:T(4,128)} %bitcast.23, s32[256]{0:T(256)} %rows_in.1, s32[2,128]{1,0:T(2,128)} %bitcast.25, f32[1,256]{1,0:T(1,128)} %bitcast.26, ...), custom_call_target="tpu_custom_call" | custom-call | flops 4000000000 | bytes 4000000 | tf_op jit(solution)/shard_map/pallas_call | solution.py:600
  75.8 0.0 copy-start
  75.8 2.3 %copy.21 = bf16[16,128,256]{2,1,0:T(8,128)(2,1)} copy(bf16[16,128,256]{2,1,0:T(8,128)(2,1)} %get-tuple-element.8) | data formatting | bytes 2097152
  78.1 0.0 copy-done
  78.1 0.7 copy.22
Async XLA Ops:
  75.8 2.3 %copy-start = (bf16[1024,128]{1,0:T(8,128)(2,1)S(1)}, bf16[1024,128]{1,0:T(8,128)(2,1)}, u32[]{:S(2)}) copy-start(bf16[1024,128]{1,0:T(8,128)(2,1)} %get-tuple-element.5) | copy-start | bytes 786436

commit v6 on v5

--- a/solution.py
+++ b/solution.py
@@ -9,7 +9,7 @@
 BF = jnp.bfloat16
 NT = (((1,), (1,)), ((), ()))
 
-SIZES = (8, 8, 4, 4, 6, 16, 16, 6, 6, 24, 16, 16, 6, 6, 3)
+SIZES = (8, 8, 4, 4, 6, 1, 1, 6, 6, 24, 1, 1, 6, 6, 3)
 RZ, XZ, XM, XF, WT, BA, BB, AX, BY, AL, LL, RR, LX, R4, UP = (
     sum(SIZES[:i]) for i in range(len(SIZES))
 )
@@ -37,13 +37,13 @@
 
 
 def kernel(
-    hom, pair_in, resm_in, rows_in, rowv_in, fscale_in, wq, wk, wv, wg, gb_in, wo, pgain_in, bw_in,
+    hom, pair_in, resm_in, rows_in, fscale_in, wq, wk, wv, wg, gb_in, wo, pgain_in, bw_in,
     cscale_in, p1_in, p2_in, ow_in,
-    out_al, out_pair,
-    xin, pair, resm, rows, rowv, fscale, gb, pgain, bw, cscale, p1, p2, ow,
+    out_al, out_update,
+    xin, pair, resm, rows, fscale, gb, pgain, bw, cscale, p1, p2, ow,
     xn, relay, wbuf, pn, bt, bg, wkn, wqvg, kb, qt, vt, gate, biasb, gbt, cm, wst, al, right, sndf, snd, lraw, rraw, scr, lb, rb,
-    bscr, ub, ubf, urecv,
-    ssem, rsem, lsem, osem,
+    bscr, ub, ubf,
+    ssem, rsem, lsem, osem, usem,
 ):
     seq = lax.axis_index("seq")
     ri = lax.axis_index("ri")
@@ -161,7 +161,6 @@
         (wo, wbuf.at[rj, pl.ds(256, 64)]),
         (resm_in, resm),
         (rows_in, rows),
-        (rowv_in, rowv),
         (gb_in, gb),
         (cscale_in, cscale),
         (p1_in, p1),
@@ -189,10 +188,6 @@
         greet(dev)
 
     def greet_right(n):
-        @pl.when(jnp.logical_not(to_self(n)))
-        def _():
-            greet(right_to(n))
-
         @pl.when(jnp.logical_not(from_self(n)))
         def _():
             greet(right_from(n))
@@ -208,7 +203,7 @@
 
     lax.fori_loop(0, 4, norm_x, 0)
 
-    pl.semaphore_wait(barrier, 65 - 2 * diagonal.astype(jnp.int32))
+    pl.semaphore_wait(barrier, 49 - diagonal.astype(jnp.int32))
 
     def send_x(s):
         rcopy(xn.at[s, ri, pl.ds(0, 64)], relay.at[0, s], RZ + s * 2, up).start()
@@ -237,8 +232,8 @@
     for half in range(2):
         bg[half, zl, x, rj] = bt[pl.ds(half * 32, 32), :].astype(BF)
     def send_bias(n):
-        rcopy(bg.at[0, zl, x, rj], bg.at[0, zl, x, rj], BA + n, in_zy(n)).start()
-        rcopy(bg.at[1, zl, x, rj], bg.at[1, zl, x, rj], BB + n, in_zx(n)).start()
+        rcopy(bg.at[0, zl, x, rj], bg.at[0, zl, x, rj], BA, in_zy(n)).start()
+        rcopy(bg.at[1, zl, x, rj], bg.at[1, zl, x, rj], BB, in_zx(n)).start()
 
     each(1, 16, send_bias)
     relay_x(0)
@@ -249,12 +244,9 @@
     ring_pass(
         wbuf.at[behind(rj, 1)], wbuf.at[ahead(rj, 1)], w_lower, w_upper, WT, plus_y, minus_y
     )
-    def came_bias(n):
-        dz, d = lax.div(n, 4), lax.rem(n, 4)
-        arrived(bg.at[0, behind(zl, dz), x, behind(rj, d)], BA + n)
-        arrived(bg.at[1, behind(zl, dz), behind(x, d), rj], BB + n)
-
-    each(1, 16, came_bias)
+    fifteen, sixteen = bscr.at[0, pl.ds(0, 240)], bscr.at[0]
+    arrived(fifteen, BA)
+    arrived(fifteen, BB)
     b_lower, b_upper = first(2), second(2)
     ring_start(bg.at[0, :, x], b_lower, b_upper, AX, plus_x, minus_x)
     ring_start(bg.at[1, :, :, rj], b_lower, b_upper, BY, plus_y, minus_y)
@@ -280,7 +272,6 @@
     ).astype(F32).astype(BF)
     p1t = p1[...]
     p2r = jnp.concatenate([p2[...]] * 4, 0)
-    total = jnp.maximum(jnp.sum(rowv[...].astype(F32)), 1.0)
 
     relay_x(3)
 
@@ -337,8 +328,7 @@
         return carry
 
     lax.fori_loop(0, 4, near_rows, 0)
-    lax.fori_loop(0, 4, far_rows, 0)
-    lax.fori_loop(0, 4, last_rows, 0)
+    lax.fori_loop(0, 2, far_rows, 0)
     ring_end(
         bg.at[0, :, behind(x, 1)], bg.at[0, :, ahead(x, 1)], bg.at[0, :, ahead(x, 2)],
         b_lower, b_upper, AX,
@@ -357,6 +347,7 @@
     lane8 = lax.div(lax.broadcasted_iota(jnp.int32, (8, 128), 1), 32)
 
     def attend(s, carry):
+        last_rows(s, carry)
         key = kb[s].reshape(512, 256)
         value = jnp.concatenate([vt[s, b] for b in range(4)], 1)
         query = qt[s]
@@ -384,7 +375,7 @@
         al[s] = result
         pltpu.make_async_copy(al.at[s], out_al.at[rj * 4 + s], osem.at[s]).start()
 
-        @pl.when(s < 2)
+        @pl.when(s < 3)
         def _():
             start_out(s)
 
@@ -404,6 +395,11 @@
                 rtile = jnp.where(lane8 == k, right[pl.ds(y * 32 + k, 8, stride=4), :], rtile)
             sndf[y, pl.ds(pl.multiple_of(s * 8, 8), 8), :] = ltile
             sndf[y, pl.ds(pl.multiple_of(32 + s * 8, 8), 8), :] = rtile
+
+        @pl.when(s < 2)
+        def _():
+            far_rows(s + 2, carry)
+
         return carry
 
     a_lower, a_upper = first(64), second(64)
@@ -429,24 +425,20 @@
 
     def send_sides(n):
         rcopy(
-            snd.at[ahead(rj, lax.rem(n, 4)), pl.ds(0, 32)], lraw.at[zl, rj], LL + n, in_zy(n)
+            snd.at[ahead(rj, lax.rem(n, 4)), pl.ds(0, 32)], lraw.at[zl, rj], LL, in_zy(n)
         ).start()
 
     each(1, 16, send_sides)
-
-    def right_copy(n):
-        return rcopy(
-            snd.at[lax.div(n, 4), pl.ds(32, 32)], rraw.at[zl, rj], RR + zl * 4 + rj, right_to(n),
-            RR + n,
-        )
 
     def send_right(n):
         @pl.when(jnp.logical_not(to_self(n)))
         def _():
-            right_copy(n).start()
+            rcopy(
+                snd.at[lax.div(n, 4), pl.ds(32, 32)], rraw.at[zl, rj], RR, right_to(n)
+            ).start()
 
     each(0, 16, send_right)
-    start_out(2)
+    each(0, 2, pass_out)
     start_out(3)
     lraw[zl, rj] = snd[rj, 0:32]
 
@@ -454,13 +446,19 @@
     def _():
         rraw[zl, rj] = snd[x, 32:64]
 
-    def came_left(n):
-        arrived(lraw.at[behind(zl, lax.div(n, 4)), behind(rj, lax.rem(n, 4))], LL + n)
-
-    def came_right(n):
-        @pl.when(jnp.logical_not(from_self(n)))
-        def _():
-            arrived(rraw.at[lax.div(n, 4), lax.rem(n, 4)], RR + n)
+    def drain_head(s):
+        for half in range(2):
+            left_here(relay.at[half, s], RZ + s * 2 + half)
+            left_here(relay.at[half, s], XZ + s * 2 + half)
+        left_here(xn.at[s, ri], XM + s)
+        left_here(xn.at[s, opp], XF + s)
+
+    each(0, 4, drain_head)
+    left_here(fifteen, BA)
+    left_here(fifteen, BB)
+    ring_sent(wbuf.at[rj], w_lower, w_upper, WT)
+    ring_sent(bg.at[0, :, x], b_lower, b_upper, AX)
+    ring_sent(bg.at[1, :, :, rj], b_lower, b_upper, BY)
 
     def regroup(raw, buf, place):
         def step(t):
@@ -473,10 +471,18 @@
         each(0, 4, step)
 
     q_lower, q_upper = first(4), second(4)
-    each(1, 16, came_left)
+    arrived(fifteen, LL)
     regroup(lraw, lb, x)
     ring_start(lb.at[:, x], q_lower, q_upper, LX, plus_x, minus_x)
-    each(0, 16, came_right)
+
+    @pl.when(diagonal)
+    def _():
+        arrived(fifteen, RR)
+
+    @pl.when(jnp.logical_not(diagonal))
+    def _():
+        arrived(sixteen, RR)
+
     regroup(rraw, rb, rj)
     ring_start(rb.at[:, rj], q_lower, q_upper, R4, plus_y, minus_y)
     ring_pass(
@@ -485,7 +491,7 @@
     ring_pass(
         rb.at[:, behind(rj, 1)], rb.at[:, ahead(rj, 1)], q_lower, q_upper, R4, plus_y, minus_y
     )
-    each(0, 4, pass_out)
+    each(2, 4, pass_out)
     ring_end(
         lb.at[:, behind(x, 1)], lb.at[:, ahead(x, 1)], lb.at[:, ahead(x, 2)], q_lower, q_upper, LX
     )
@@ -518,35 +524,30 @@
                 )
         return carry
 
-    def for_peer(d):
+    def in_order(t):
+        return jnp.where(t == 0, 2, jnp.where(t == 1, 1, t + 1))
+
+    def for_peer(t):
+        d = in_order(t)
         peer = ahead(rj, d)
         lax.fori_loop(0, 2, lambda u, carry: product(peer, u, carry), 0)
         ubf[peer] = ub[peer].astype(BF)
 
-        @pl.when(d < 4)
+        @pl.when(t < 3)
         def _():
             update_copy(d).start()
 
     def update_copy(d):
         peer = ahead(rj, d)
-        return rcopy(ubf.at[peer], urecv.at[rj], UP + d - 1, {"rj": peer})
-
-    each(1, 5, for_peer)
-    urecv[rj] = ubf[rj]
-    scale = 1.0 / total
-    for d in (1, 2, 3):
-        arrived(urecv.at[behind(rj, d)], UP + d - 1)
-    out_pair[...] = (
-        pair[...].astype(F32) + urecv[...].reshape(1024, 128).astype(F32) * scale
-    ).astype(BF)
+        return rcopy(ubf.at[peer], out_update.at[rj], UP + d - 1, {"rj": peer})
+
+    each(0, 4, for_peer)
+    keep_own = pltpu.make_async_copy(ubf.at[rj], out_update.at[rj], usem)
+    keep_own.start()
+    each(1, 4, lambda d: arrived(out_update.at[behind(rj, d)], UP + d - 1))
 
     def drain(s):
         pltpu.make_async_copy(al.at[s], out_al.at[rj * 4 + s], osem.at[s]).wait()
-        for half in range(2):
-            left_here(relay.at[half, s], RZ + s * 2 + half)
-            left_here(relay.at[half, s], XZ + s * 2 + half)
-        left_here(xn.at[s, ri], XM + s)
-        left_here(xn.at[s, opp], XF + s)
         ring_end(
             out(s, behind(rj, 1)), out(s, ahead(rj, 1)), out(s, ahead(rj, 2)), a_lower, a_upper,
             AL + s * 6,
@@ -554,26 +555,42 @@
         ring_sent(al.at[s], a_lower, a_upper, AL + s * 6)
 
     each(0, 4, drain)
-    ring_sent(wbuf.at[rj], w_lower, w_upper, WT)
-    ring_sent(bg.at[0, :, x], b_lower, b_upper, AX)
-    ring_sent(bg.at[1, :, :, rj], b_lower, b_upper, BY)
     ring_sent(lb.at[:, x], q_lower, q_upper, LX)
     ring_sent(rb.at[:, rj], q_lower, q_upper, R4)
-
-    def drain_small(n):
-        left_here(bg.at[0, zl, x, rj], BA + n)
-        left_here(bg.at[1, zl, x, rj], BB + n)
-        left_here(lraw.at[zl, rj], LL + n)
-
-    each(1, 16, drain_small)
-
-    def drain_right(n):
-        @pl.when(jnp.logical_not(to_self(n)))
-        def _():
-            left_here(rraw.at[zl, rj], RR + n)
-
-    each(0, 16, drain_right)
+    left_here(fifteen, LL)
+
+    @pl.when(diagonal)
+    def _():
+        left_here(fifteen, RR)
+
+    @pl.when(jnp.logical_not(diagonal))
+    def _():
+        left_here(sixteen, RR)
+
     each(1, 4, lambda d: left_here(ubf.at[ahead(rj, d)], UP + d - 1))
+    keep_own.wait()
+
+
+def finish(al_in, update_in, pair_in, rowv_in, al_out, pair_out, update, pair, rowv, result, sem):
+    whole = pltpu.make_async_copy(al_in, al_out, sem.at[0])
+    whole.start()
+    parts = [
+        pltpu.make_async_copy(update_in, update, sem.at[1]),
+        pltpu.make_async_copy(pair_in, pair, sem.at[2]),
+        pltpu.make_async_copy(rowv_in, rowv, sem.at[3]),
+    ]
+    for part in parts:
+        part.start()
+    for part in parts:
+        part.wait()
+    scale = 1.0 / jnp.maximum(jnp.sum(rowv[...].astype(F32)), 1.0)
+    result[...] = (
+        pair[...].astype(F32) + update[...].reshape(1024, 128).astype(F32) * scale
+    ).astype(BF)
+    back = pltpu.make_async_copy(result, pair_out, sem.at[4])
+    back.start()
+    back.wait()
+    whole.wait()
 
 
 def on_device(
@@ -595,22 +612,20 @@
     second_cross_projector,
     outer_weight,
 ):
-    vmem = pl.BlockSpec(memory_space=pltpu.VMEM)
     hbm = pl.BlockSpec(memory_space=pl.ANY)
-    alignment_output, pair_rows = pl.pallas_call(
+    gathered, update = pl.pallas_call(
         kernel,
         out_shape=(
             jax.ShapeDtypeStruct((16, 128, 256), BF),
-            jax.ShapeDtypeStruct((1024, 128), BF),
+            jax.ShapeDtypeStruct((4, 256, 128), BF),
         ),
-        in_specs=[hbm] * 18,
-        out_specs=(hbm, vmem),
+        in_specs=[hbm] * 17,
+        out_specs=(hbm, hbm),
         scratch_shapes=[
             pltpu.VMEM((4, 128, 256), BF),
             pltpu.VMEM((1024, 128), BF),
             pltpu.VMEM((4, 128), jnp.int32),
             pltpu.SMEM((256,), jnp.int32),
-            pltpu.VMEM((2, 128), jnp.int32),
             pltpu.VMEM((1, 256), F32),
             pltpu.VMEM((1, 256), F32),
             pltpu.VMEM((1, 128), F32),
@@ -647,11 +662,11 @@
             pltpu.VMEM((2, 256, 256), BF),
             pltpu.VMEM((4, 256, 128), F32),
             pltpu.VMEM((4, 256, 128), BF),
-            pltpu.VMEM((4, 256, 128), BF),
             pltpu.SemaphoreType.DMA((COUNT,)),
             pltpu.SemaphoreType.DMA((COUNT,)),
-            pltpu.SemaphoreType.DMA((18,)),
+            pltpu.SemaphoreType.DMA((17,)),
             pltpu.SemaphoreType.DMA((4,)),
+            pltpu.SemaphoreType.DMA,
         ],
         compiler_params=pltpu.CompilerParams(
             collective_id=0, has_side_effects=True, vmem_limit_bytes=60 * 1024 * 1024
@@ -664,7 +679,6 @@
         pairwise_state.reshape(1024, 128),
         residue_mask.reshape(4, 128),
         alignment_row_mask,
-        alignment_row_mask.reshape(2, 128),
         focus_layer_scale.reshape(1, 256),
         asking_projector.T,
         lookup_projector.T,
@@ -679,6 +693,23 @@
         second_cross_projector.T,
         outer_weight,
     )
+    alignment_output, pair_rows = pl.pallas_call(
+        finish,
+        out_shape=(
+            jax.ShapeDtypeStruct((16, 128, 256), BF),
+            jax.ShapeDtypeStruct((1024, 128), BF),
+        ),
+        in_specs=[hbm] * 4,
+        out_specs=(hbm, hbm),
+        scratch_shapes=[
+            pltpu.VMEM((4, 256, 128), BF),
+            pltpu.VMEM((1024, 128), BF),
+            pltpu.VMEM((2, 128), jnp.int32),
+            pltpu.VMEM((1024, 128), BF),
+            pltpu.SemaphoreType.DMA((5,)),
+        ],
+        compiler_params=pltpu.CompilerParams(vmem_limit_bytes=60 * 1024 * 1024),
+    )(gathered, update, pairwise_state.reshape(1024, 128), alignment_row_mask.reshape(2, 128))
     return alignment_output, pair_rows.reshape(128, 8, 128)
 
 

time: 79.6 us -> 108 us (1.36)
  Pallas kernels: 75.1 us -> 107 us
  local copies, waits for them, and re-layouts: 3.04 us -> 0 us
    pallas_call x0 -> x1, Pallas kernels: none -> 32.9 us  [on_device(): pl.pallas_call(finish, out_shape=(jax.ShapeDtypeStruct((16, 128, 256), BF...]
    unnamed x4 -> x0, local copies, waits for them, and re-layouts: 3.04 us -> none
where the time goes in v6:
time: 108 us
  Pallas kernels  107 us (99%)
    pallas_call x1, Pallas kernels, on_device(): pl.pallas_call(kernel, out_shape=(jax.ShapeDtypeStruct((16, 128, 256), BF...  74.3 us
    pallas_call x1, Pallas kernels, on_device(): pl.pallas_call(finish, out_shape=(jax.ShapeDtypeStruct((16, 128, 256), BF...  32.9 us

profile of v6, /device:TPU:16, one launch (start us, length us, event | category | flops | bytes accessed | tf_op | source)
XLA Modules:
  0.0 107.8 jit_solution(14952972960337613725)
XLA Ops:
  0.6 74.3 %shard_map.176 = (bf16[16,128,256]{2,1,0:T(8,128)(2,1)}, bf16[4,256,128]{2,1,0:T(8,128)(2,1)}) custom-call(bf16[16,128,256]{2,1,0:T(8,128)(2,1)} %hom.1, bf16[1024,128]{1,0:T(8,128)(2,1)} %bitcast.15, s32[4,128]{1,0:T(4,128)} %bitcast.25, s32[256]{0:T(256)} %rows_in.1, f32[1,256]{1,0:T(1,128)} %bitcast.27, bf16[64,256]{1,0:T(8,128)(2,1)} %bitcast.19, ...), custom_call_target="tpu_custom_call" | custom-call | flops 4000000000 | bytes 4000000 | tf_op jit(solution)/shard_map/pallas_call | solution.py:616
  74.9 32.9 %shard_map.177 = (bf16[16,128,256]{2,1,0:T(8,128)(2,1)}, bf16[1024,128]{1,0:T(8,128)(2,1)}) custom-call(bf16[16,128,256]{2,1,0:T(8,128)(2,1)} %get-tuple-element.6.al_in, bf16[4,256,128]{2,1,0:T(8,128)(2,1)} %get-tuple-element.7.update_in, bf16[1024,128]{1,0:T(8,128)(2,1)} %bitcast.16, s32[2,128]{1,0:T(2,128)} %bitcast.17), custom_call_target="tpu_custom_call" | custom-call | tf_op jit(solution)/shard_map/pallas_call | solution.py:696

commit v7 on v6

--- a/solution.py
+++ b/solution.py
@@ -42,7 +42,7 @@
     out_al, out_update,
     xin, pair, resm, rows, fscale, gb, pgain, bw, cscale, p1, p2, ow,
     xn, relay, wbuf, pn, bt, bg, wkn, wqvg, kb, qt, vt, gate, biasb, gbt, cm, wst, al, right, sndf, snd, lraw, rraw, scr, lb, rb,
-    bscr, ub, ubf,
+    bscr, ub, ubf, ugot,
     ssem, rsem, lsem, osem, usem,
 ):
     seq = lax.axis_index("seq")
@@ -372,8 +372,7 @@
         attended = (jnp.concatenate(parts, 0) * gate[s]).astype(BF)
         attended = nt(e128, attended).astype(BF)
         result = (xin[s].astype(F32) + mm(attended, weight(4))).astype(BF)
-        al[s] = result
-        pltpu.make_async_copy(al.at[s], out_al.at[rj * 4 + s], osem.at[s]).start()
+        al[rj, s] = result
 
         @pl.when(s < 3)
         def _():
@@ -405,13 +404,13 @@
     a_lower, a_upper = first(64), second(64)
 
     def out(s, source):
-        return out_al.at[source * 4 + s]
+        return al.at[source, s]
 
     def start_out(s):
         for i, (part, dev) in enumerate(
             ((a_lower, plus_y), (a_upper, minus_y), (a_upper, plus_y), (a_lower, minus_y))
         ):
-            rcopy(part(al.at[s]), part(out(s, rj)), AL + s * 6 + i, dev).start()
+            rcopy(part(out(s, rj)), part(out(s, rj)), AL + s * 6 + i, dev).start()
 
     def pass_out(s):
         ring_pass(
@@ -539,22 +538,26 @@
 
     def update_copy(d):
         peer = ahead(rj, d)
-        return rcopy(ubf.at[peer], out_update.at[rj], UP + d - 1, {"rj": peer})
+        return rcopy(ubf.at[peer], ugot.at[rj], UP + d - 1, {"rj": peer})
 
     each(0, 4, for_peer)
-    keep_own = pltpu.make_async_copy(ubf.at[rj], out_update.at[rj], usem)
-    keep_own.start()
-    each(1, 4, lambda d: arrived(out_update.at[behind(rj, d)], UP + d - 1))
+    ugot[rj] = ubf[rj]
+    each(1, 4, lambda d: arrived(ugot.at[behind(rj, d)], UP + d - 1))
+    keep = pltpu.make_async_copy(ugot, out_update, usem)
+    keep.start()
+
+    def write_out(s):
+        return pltpu.make_async_copy(al.at[:, s], out_al.at[:, s], osem.at[s])
 
     def drain(s):
-        pltpu.make_async_copy(al.at[s], out_al.at[rj * 4 + s], osem.at[s]).wait()
         ring_end(
             out(s, behind(rj, 1)), out(s, ahead(rj, 1)), out(s, ahead(rj, 2)), a_lower, a_upper,
             AL + s * 6,
         )
-        ring_sent(al.at[s], a_lower, a_upper, AL + s * 6)
+        write_out(s).start()
 
     each(0, 4, drain)
+    each(0, 4, lambda s: ring_sent(out(s, rj), a_lower, a_upper, AL + s * 6))
     ring_sent(lb.at[:, x], q_lower, q_upper, LX)
     ring_sent(rb.at[:, rj], q_lower, q_upper, R4)
     left_here(fifteen, LL)
@@ -568,29 +571,34 @@
         left_here(sixteen, RR)
 
     each(1, 4, lambda d: left_here(ubf.at[ahead(rj, d)], UP + d - 1))
-    keep_own.wait()
-
-
-def finish(al_in, update_in, pair_in, rowv_in, al_out, pair_out, update, pair, rowv, result, sem):
-    whole = pltpu.make_async_copy(al_in, al_out, sem.at[0])
-    whole.start()
-    parts = [
-        pltpu.make_async_copy(update_in, update, sem.at[1]),
-        pltpu.make_async_copy(pair_in, pair, sem.at[2]),
-        pltpu.make_async_copy(rowv_in, rowv, sem.at[3]),
-    ]
-    for part in parts:
-        part.start()
-    for part in parts:
-        part.wait()
+    keep.wait()
+    each(0, 4, lambda s: write_out(s).wait())
+
+
+def finish(
+    al_in, update_in, pair_in, rowv_in, al_out, pair_out, al, update, pair, rowv, result, sem, back
+):
+    inward = [
+        pltpu.make_async_copy(update_in, update, sem.at[0]),
+        pltpu.make_async_copy(pair_in, pair, sem.at[1]),
+        pltpu.make_async_copy(rowv_in, rowv, sem.at[2]),
+    ] + [pltpu.make_async_copy(al_in.at[k], al.at[k], sem.at[3 + k]) for k in range(4)]
+    outward = [pltpu.make_async_copy(al.at[k], al_out.at[k], back.at[k]) for k in range(4)]
+    outward.append(pltpu.make_async_copy(result, pair_out, back.at[4]))
+    for copy in inward:
+        copy.start()
+    for k in range(3):
+        inward[k].wait()
     scale = 1.0 / jnp.maximum(jnp.sum(rowv[...].astype(F32)), 1.0)
     result[...] = (
         pair[...].astype(F32) + update[...].reshape(1024, 128).astype(F32) * scale
     ).astype(BF)
-    back = pltpu.make_async_copy(result, pair_out, sem.at[4])
-    back.start()
-    back.wait()
-    whole.wait()
+    outward[4].start()
+    for k in range(4):
+        inward[3 + k].wait()
+        outward[k].start()
+    for copy in outward:
+        copy.wait()
 
 
 def on_device(
@@ -616,7 +624,7 @@
     gathered, update = pl.pallas_call(
         kernel,
         out_shape=(
-            jax.ShapeDtypeStruct((16, 128, 256), BF),
+            jax.ShapeDtypeStruct((4, 4, 128, 256), BF),
             jax.ShapeDtypeStruct((4, 256, 128), BF),
         ),
         in_specs=[hbm] * 17,
@@ -650,7 +658,7 @@
             pltpu.VMEM((256, 128), F32),
             pltpu.VMEM((4, 128, 128), F32),
             pltpu.VMEM((512, 256), BF),
-            pltpu.VMEM((4, 128, 256), BF),
+            pltpu.VMEM((4, 4, 128, 256), BF),
             pltpu.VMEM((128, 128), F32),
             pltpu.VMEM((4, 64, 128), F32),
             pltpu.VMEM((4, 64, 128), BF),
@@ -661,6 +669,7 @@
             pltpu.VMEM((8, 4, 4, 16, 128), BF),
             pltpu.VMEM((2, 256, 256), BF),
             pltpu.VMEM((4, 256, 128), F32),
+            pltpu.VMEM((4, 256, 128), BF),
             pltpu.VMEM((4, 256, 128), BF),
             pltpu.SemaphoreType.DMA((COUNT,)),
             pltpu.SemaphoreType.DMA((COUNT,)),
@@ -696,21 +705,23 @@
     alignment_output, pair_rows = pl.pallas_call(
         finish,
         out_shape=(
-            jax.ShapeDtypeStruct((16, 128, 256), BF),
+            jax.ShapeDtypeStruct((4, 4, 128, 256), BF),
             jax.ShapeDtypeStruct((1024, 128), BF),
         ),
         in_specs=[hbm] * 4,
         out_specs=(hbm, hbm),
         scratch_shapes=[
+            pltpu.VMEM((4, 4, 128, 256), BF),
             pltpu.VMEM((4, 256, 128), BF),
             pltpu.VMEM((1024, 128), BF),
             pltpu.VMEM((2, 128), jnp.int32),
             pltpu.VMEM((1024, 128), BF),
+            pltpu.SemaphoreType.DMA((7,)),
             pltpu.SemaphoreType.DMA((5,)),
         ],
         compiler_params=pltpu.CompilerParams(vmem_limit_bytes=60 * 1024 * 1024),
     )(gathered, update, pairwise_state.reshape(1024, 128), alignment_row_mask.reshape(2, 128))
-    return alignment_output, pair_rows.reshape(128, 8, 128)
+    return alignment_output.reshape(16, 128, 256), pair_rows.reshape(128, 8, 128)
 
 
 def solution(mesh):

time: 108 us -> 78.5 us (0.73)
  Pallas kernels: 107 us -> 77.6 us
    pallas_call x2, Pallas kernels: 107 us -> 77.6 us  [the longest x1 75.2 us: on_device(): pl.pallas_call(kernel, out_shape=(jax.ShapeDtypeStruct((4, 4, 128, 256),...]
where the time goes in v7:
time: 78.5 us; the launch traced here: 78.2 us
  Pallas kernels  77.6 us (99%)
    pallas_call x1, Pallas kernels, on_device(): pl.pallas_call(kernel, out_shape=(jax.ShapeDtypeStruct((4, 4, 128, 256),...  75.2 us
    pallas_call x1, Pallas kernels, on_device(): pl.pallas_call(finish, out_shape=(jax.ShapeDtypeStruct((4, 4, 128, 256),...  2.43 us

profile of v7, /device:TPU:16, one launch (start us, length us, event | category | flops | bytes accessed | tf_op | source)
XLA Modules:
  0.0 78.2 jit_solution(941551453003641064)
XLA Ops:
  0.6 75.2 %shard_map.176 = (bf16[4,4,128,256]{3,2,1,0:T(8,128)(2,1)}, bf16[4,256,128]{2,1,0:T(8,128)(2,1)}) custom-call(bf16[16,128,256]{2,1,0:T(8,128)(2,1)} %hom.1, bf16[1024,128]{1,0:T(8,128)(2,1)} %bitcast.16, s32[4,128]{1,0:T(4,128)} %bitcast.27, s32[256]{0:T(256)} %rows_in.1, f32[1,256]{1,0:T(1,128)} %bitcast.29, bf16[64,256]{1,0:T(8,128)(2,1)} %bitcast.21, ...), custom_call_target="tpu_custom_call" | custom-call | flops 4000000000 | bytes 4000000 | tf_op jit(solution)/shard_map/pallas_call | solution.py:624
  75.8 2.4 %shard_map.177 = (bf16[4,4,128,256]{3,2,1,0:T(8,128)(2,1)}, bf16[1024,128]{1,0:T(8,128)(2,1)}) custom-call(bf16[4,4,128,256]{3,2,1,0:T(8,128)(2,1)} %get-tuple-element.6.al_in, bf16[4,256,128]{2,1,0:T(8,128)(2,1)} %get-tuple-element.7.update_in, bf16[1024,128]{1,0:T(8,128)(2,1)} %bitcast.17, s32[2,128]{1,0:T(2,128)} %bitcast.18), custom_call_target="tpu_custom_call" | custom-call | tf_op jit(solution)/shard_map/pallas_call | solution.py:705

commit v8 on v7

--- a/solution.py
+++ b/solution.py
@@ -244,7 +244,7 @@
     ring_pass(
         wbuf.at[behind(rj, 1)], wbuf.at[ahead(rj, 1)], w_lower, w_upper, WT, plus_y, minus_y
     )
-    fifteen, sixteen = bscr.at[0, pl.ds(0, 240)], bscr.at[0]
+    fifteen, sixteen = bscr.at[0, 0, pl.ds(0, 240)], bscr.at[0, 0]
     arrived(fifteen, BA)
     arrived(fifteen, BB)
     b_lower, b_upper = first(2), second(2)
@@ -346,8 +346,7 @@
 
     lane8 = lax.div(lax.broadcasted_iota(jnp.int32, (8, 128), 1), 32)
 
-    def attend(s, carry):
-        last_rows(s, carry)
+    def heads(s):
         key = kb[s].reshape(512, 256)
         value = jnp.concatenate([vt[s, b] for b in range(4)], 1)
         query = qt[s]
@@ -369,15 +368,12 @@
             scale = 1.0 / summed[64:65]
             parts.append(summed[0:32, 0:128] * scale[:, 0:128])
             parts.append(summed[32:64, 128:256] * scale[:, 128:256])
-        attended = (jnp.concatenate(parts, 0) * gate[s]).astype(BF)
+        return (jnp.concatenate(parts, 0) * gate[s]).astype(BF)
+
+    def project(s, attended):
         attended = nt(e128, attended).astype(BF)
         result = (xin[s].astype(F32) + mm(attended, weight(4))).astype(BF)
         al[rj, s] = result
-
-        @pl.when(s < 3)
-        def _():
-            start_out(s)
-
         on = norm(result.astype(F32), cscale[...])
         keep = cm[ri] * rows[seq * 16 + rj * 4 + s].astype(F32)
         on = (on * jnp.concatenate([keep, keep], 1)).astype(BF)
@@ -395,11 +391,20 @@
             sndf[y, pl.ds(pl.multiple_of(s * 8, 8), 8), :] = ltile
             sndf[y, pl.ds(pl.multiple_of(32 + s * 8, 8), 8), :] = rtile
 
+    def attend(s, before):
+        last_rows(s, 0)
+        attended = heads(s)
+        project(lax.rem(s + 3, 4), before)
+
+        @pl.when(s > 0)
+        def _():
+            start_out(s - 1)
+
         @pl.when(s < 2)
         def _():
-            far_rows(s + 2, carry)
-
-        return carry
+            far_rows(s + 2, 0)
+
+        return attended
 
     a_lower, a_upper = first(64), second(64)
 
@@ -418,7 +423,7 @@
             plus_y, minus_y,
         )
 
-    lax.fori_loop(0, 4, attend, 0)
+    project(3, lax.fori_loop(0, 4, attend, jnp.zeros((256, 128), BF)))
 
     snd[...] = sndf[...].astype(BF)
 
@@ -501,16 +506,16 @@
 
     lane128 = lax.div(lax.broadcasted_iota(jnp.int32, (128, 128), 1), 32)
 
-    def product(peer, u, carry):
+    def product(peer, u):
         turned = nt(e128, rb[peer * 2 + u].reshape(256, 128)).astype(BF)
         for k in range(8):
             outer = mm(turned, lb[k].reshape(256, 128)).astype(BF)
             for j in range(4):
-                bscr[j // 2, pl.ds(k * 32, 32), pl.ds((j % 2) * 128, 128)] = outer[
+                bscr[u, j // 2, pl.ds(k * 32, 32), pl.ds((j % 2) * 128, 128)] = outer[
                     j * 32 : j * 32 + 32
                 ]
         for jp in range(2):
-            wide = mm(wst[...], bscr[jp])
+            wide = mm(wst[...], bscr[u, jp])
             for half in range(2):
                 c = half * 128
                 mixed = wide[0:128, c : c + 128]
@@ -521,7 +526,6 @@
                 ub[peer, pl.ds(u * 4 + jp * 2 + half, 32, stride=8), :] = nt(
                     pick, mixed.astype(BF)
                 )
-        return carry
 
     def in_order(t):
         return jnp.where(t == 0, 2, jnp.where(t == 1, 1, t + 1))
@@ -529,7 +533,8 @@
     def for_peer(t):
         d = in_order(t)
         peer = ahead(rj, d)
-        lax.fori_loop(0, 2, lambda u, carry: product(peer, u, carry), 0)
+        for u in range(2):
+            product(peer, u)
         ubf[peer] = ub[peer].astype(BF)
 
         @pl.when(t < 3)
@@ -667,7 +672,7 @@
             pltpu.VMEM((128, 128), F32),
             pltpu.VMEM((8, 4, 4, 16, 128), BF),
             pltpu.VMEM((8, 4, 4, 16, 128), BF),
-            pltpu.VMEM((2, 256, 256), BF),
+            pltpu.VMEM((2, 2, 256, 256), BF),
             pltpu.VMEM((4, 256, 128), F32),
             pltpu.VMEM((4, 256, 128), BF),
             pltpu.VMEM((4, 256, 128), BF),

time: 78.5 us -> 78.3 us (level)
  no operation moved by 1% of the time
where the time goes in v8:
time: 78.3 us; the launch traced here: 78 us
  Pallas kernels  77.4 us (99%)
    pallas_call x1, Pallas kernels, on_device(): pl.pallas_call(kernel, out_shape=(jax.ShapeDtypeStruct((4, 4, 128, 256),...  74.9 us
    pallas_call x1, Pallas kernels, on_device(): pl.pallas_call(finish, out_shape=(jax.ShapeDtypeStruct((4, 4, 128, 256),...  2.43 us

profile of v8, /device:TPU:16, one launch (start us, length us, event | category | flops | bytes accessed | tf_op | source)
XLA Modules:
  0.0 78.0 jit_solution(4748793404065195895)
XLA Ops:
  0.6 74.9 %shard_map.176 = (bf16[4,4,128,256]{3,2,1,0:T(8,128)(2,1)}, bf16[4,256,128]{2,1,0:T(8,128)(2,1)}) custom-call(bf16[16,128,256]{2,1,0:T(8,128)(2,1)} %hom.1, bf16[1024,128]{1,0:T(8,128)(2,1)} %bitcast.16, s32[4,128]{1,0:T(4,128)} %bitcast.27, s32[256]{0:T(256)} %rows_in.1, f32[1,256]{1,0:T(1,128)} %bitcast.29, bf16[64,256]{1,0:T(8,128)(2,1)} %bitcast.21, ...), custom_call_target="tpu_custom_call" | custom-call | flops 4000000000 | bytes 4000000 | tf_op jit(solution)/shard_map/pallas_call | solution.py:629
  75.6 2.4 %shard_map.177 = (bf16[4,4,128,256]{3,2,1,0:T(8,128)(2,1)}, bf16[1024,128]{1,0:T(8,128)(2,1)}) custom-call(bf16[4,4,128,256]{3,2,1,0:T(8,128)(2,1)} %get-tuple-element.6.al_in, bf16[4,256,128]{2,1,0:T(8,128)(2,1)} %get-tuple-element.7.update_in, bf16[1024,128]{1,0:T(8,128)(2,1)} %bitcast.17, s32[2,128]{1,0:T(2,128)} %bitcast.18), custom_call_target="tpu_custom_call" | custom-call | tf_op jit(solution)/shard_map/pallas_call | solution.py:710

commit v9 on v8

--- a/solution.py
+++ b/solution.py
@@ -203,26 +203,6 @@
 
     lax.fori_loop(0, 4, norm_x, 0)
 
-    pl.semaphore_wait(barrier, 49 - diagonal.astype(jnp.int32))
-
-    def send_x(s):
-        rcopy(xn.at[s, ri, pl.ds(0, 64)], relay.at[0, s], RZ + s * 2, up).start()
-        rcopy(xn.at[s, ri, pl.ds(64, 64)], relay.at[1, s], RZ + s * 2 + 1, down).start()
-        rcopy(xn.at[s, ri], xn.at[s, ri], XM + s, {"ri": mate}).start()
-
-    def relay_x(s):
-        arrived(relay.at[0, s], RZ + s * 2)
-        rcopy(relay.at[0, s], xn.at[s, ri_down, pl.ds(0, 64)], XZ + s * 2, up).start()
-        arrived(relay.at[1, s], RZ + s * 2 + 1)
-        rcopy(relay.at[1, s], xn.at[s, ri_up, pl.ds(64, 64)], XZ + s * 2 + 1, down).start()
-
-    for s in range(4):
-        send_x(s)
-    for k in range(5, 10):
-        local(k).wait()
-    w_lower, w_upper = first(160), second(160)
-    ring_start(wbuf.at[rj], w_lower, w_upper, WT, plus_y, minus_y)
-
     for k in range(2, 5):
         local(k).wait()
     pn[...] = norm(pair[...].astype(F32), pgain[...]).astype(BF).astype(F32)
@@ -231,26 +211,34 @@
         bt[pl.ds(j, 8, stride=8), :] = nt(bw[...], tile)
     for half in range(2):
         bg[half, zl, x, rj] = bt[pl.ds(half * 32, 32), :].astype(BF)
+
+    pl.semaphore_wait(barrier, 49 - diagonal.astype(jnp.int32))
+
+    def send_x(s):
+        rcopy(xn.at[s, ri, pl.ds(0, 64)], relay.at[0, s], RZ + s * 2, up).start()
+        rcopy(xn.at[s, ri, pl.ds(64, 64)], relay.at[1, s], RZ + s * 2 + 1, down).start()
+
+    def relay_x(s):
+        arrived(relay.at[0, s], RZ + s * 2)
+        rcopy(relay.at[0, s], xn.at[s, ri_down, pl.ds(0, 64)], XZ + s * 2, up).start()
+        arrived(relay.at[1, s], RZ + s * 2 + 1)
+        rcopy(relay.at[1, s], xn.at[s, ri_up, pl.ds(64, 64)], XZ + s * 2 + 1, down).start()
+
     def send_bias(n):
         rcopy(bg.at[0, zl, x, rj], bg.at[0, zl, x, rj], BA, in_zy(n)).start()
         rcopy(bg.at[1, zl, x, rj], bg.at[1, zl, x, rj], BB, in_zx(n)).start()
 
     each(1, 16, send_bias)
-    relay_x(0)
-    relay_x(1)
-
+    for s in range(4):
+        send_x(s)
+    for s in range(4):
+        rcopy(xn.at[s, ri], xn.at[s, ri], XM + s, {"ri": mate}).start()
+    for k in range(5, 10):
+        local(k).wait()
+    w_lower, w_upper = first(160), second(160)
+    ring_start(wbuf.at[rj], w_lower, w_upper, WT, plus_y, minus_y)
     for k in range(10, len(inward)):
         local(k).wait()
-    ring_pass(
-        wbuf.at[behind(rj, 1)], wbuf.at[ahead(rj, 1)], w_lower, w_upper, WT, plus_y, minus_y
-    )
-    fifteen, sixteen = bscr.at[0, 0, pl.ds(0, 240)], bscr.at[0, 0]
-    arrived(fifteen, BA)
-    arrived(fifteen, BB)
-    b_lower, b_upper = first(2), second(2)
-    ring_start(bg.at[0, :, x], b_lower, b_upper, AX, plus_x, minus_x)
-    ring_start(bg.at[1, :, :, rj], b_lower, b_upper, BY, plus_y, minus_y)
-    relay_x(2)
 
     row128 = lax.broadcasted_iota(jnp.int32, (128, 128), 0)
     col128 = lax.broadcasted_iota(jnp.int32, (128, 128), 1)
@@ -273,7 +261,26 @@
     p1t = p1[...]
     p2r = jnp.concatenate([p2[...]] * 4, 0)
 
+    fifteen, sixteen = bscr.at[0, 0, pl.ds(0, 240)], bscr.at[0, 0]
+    arrived(fifteen, BA)
+    arrived(fifteen, BB)
+    b_lower, b_upper = first(2), second(2)
+    ring_start(bg.at[0, :, x], b_lower, b_upper, AX, plus_x, minus_x)
+    ring_start(bg.at[1, :, :, rj], b_lower, b_upper, BY, plus_y, minus_y)
+    relay_x(0)
+    relay_x(1)
+    ring_pass(
+        wbuf.at[behind(rj, 1)], wbuf.at[ahead(rj, 1)], w_lower, w_upper, WT, plus_y, minus_y
+    )
+    relay_x(2)
     relay_x(3)
+    ring_pass(
+        bg.at[0, :, behind(x, 1)], bg.at[0, :, ahead(x, 1)], b_lower, b_upper, AX, plus_x, minus_x
+    )
+    ring_pass(
+        bg.at[1, :, :, behind(rj, 1)], bg.at[1, :, :, ahead(rj, 1)], b_lower, b_upper,
+        BY, plus_y, minus_y,
+    )
 
     ring_end(
         wbuf.at[behind(rj, 1)], wbuf.at[ahead(rj, 1)], wbuf.at[ahead(rj, 2)], w_lower, w_upper, WT
@@ -302,13 +309,6 @@
         vt[s, b] = nt(wqvg[256:512], block).astype(BF)
 
     lax.fori_loop(0, 4, own_rows, 0)
-    ring_pass(
-        bg.at[0, :, behind(x, 1)], bg.at[0, :, ahead(x, 1)], b_lower, b_upper, AX, plus_x, minus_x
-    )
-    ring_pass(
-        bg.at[1, :, :, behind(rj, 1)], bg.at[1, :, :, ahead(rj, 1)], b_lower, b_upper,
-        BY, plus_y, minus_y,
-    )
 
     def near_rows(s, carry):
         arrived(xn.at[s, mate], XM + s)

time: 78.3 us -> 76 us (0.971)
  Pallas kernels: 77.4 us -> 75 us
    pallas_call x1, Pallas kernels: 74.9 us -> 72.6 us  [on_device(): pl.pallas_call(kernel, out_shape=(jax.ShapeDtypeStruct((4, 4, 128, 256),...]
where the time goes in v9:
time: 76 us; the launch traced here: 75.6 us
  Pallas kernels  75 us (99%)
    pallas_call x1, Pallas kernels, on_device(): pl.pallas_call(kernel, out_shape=(jax.ShapeDtypeStruct((4, 4, 128, 256),...  72.6 us
    pallas_call x1, Pallas kernels, on_device(): pl.pallas_call(finish, out_shape=(jax.ShapeDtypeStruct((4, 4, 128, 256),...  2.43 us

profile of v9, /device:TPU:16, one launch (start us, length us, event | category | flops | bytes accessed | tf_op | source)
XLA Modules:
  0.0 75.6 jit_solution(3793142799006638640)
XLA Ops:
  0.6 72.6 %shard_map.176 = (bf16[4,4,128,256]{3,2,1,0:T(8,128)(2,1)}, bf16[4,256,128]{2,1,0:T(8,128)(2,1)}) custom-call(bf16[16,128,256]{2,1,0:T(8,128)(2,1)} %hom.1, bf16[1024,128]{1,0:T(8,128)(2,1)} %bitcast.16, s32[4,128]{1,0:T(4,128)} %bitcast.27, s32[256]{0:T(256)} %rows_in.1, f32[1,256]{1,0:T(1,128)} %bitcast.29, bf16[64,256]{1,0:T(8,128)(2,1)} %bitcast.21, ...), custom_call_target="tpu_custom_call" | custom-call | flops 4000000000 | bytes 4000000 | tf_op jit(solution)/shard_map/pallas_call | solution.py:629
  73.2 2.4 %shard_map.177 = (bf16[4,4,128,256]{3,2,1,0:T(8,128)(2,1)}, bf16[1024,128]{1,0:T(8,128)(2,1)}) custom-call(bf16[4,4,128,256]{3,2,1,0:T(8,128)(2,1)} %get-tuple-element.6.al_in, bf16[4,256,128]{2,1,0:T(8,128)(2,1)} %get-tuple-element.7.update_in, bf16[1024,128]{1,0:T(8,128)(2,1)} %bitcast.17, s32[2,128]{1,0:T(2,128)} %bitcast.18), custom_call_target="tpu_custom_call" | custom-call | tf_op jit(solution)/shard_map/pallas_call | solution.py:710

commit v10 on v9

--- a/solution.py
+++ b/solution.py
@@ -396,7 +396,7 @@
         attended = heads(s)
         project(lax.rem(s + 3, 4), before)
 
-        @pl.when(s > 0)
+        @pl.when(jnp.logical_and(s > 0, s < 3))
         def _():
             start_out(s - 1)
 
@@ -442,8 +442,6 @@
             ).start()
 
     each(0, 16, send_right)
-    each(0, 2, pass_out)
-    start_out(3)
     lraw[zl, rj] = snd[rj, 0:32]
 
     @pl.when(diagonal)
@@ -495,7 +493,8 @@
     ring_pass(
         rb.at[:, behind(rj, 1)], rb.at[:, ahead(rj, 1)], q_lower, q_upper, R4, plus_y, minus_y
     )
-    each(2, 4, pass_out)
+    each(2, 4, start_out)
+    each(0, 2, pass_out)
     ring_end(
         lb.at[:, behind(x, 1)], lb.at[:, ahead(x, 1)], lb.at[:, ahead(x, 2)], q_lower, q_upper, LX
     )
@@ -527,6 +526,16 @@
                     pick, mixed.astype(BF)
                 )
 
+    def write_out(s):
+        return pltpu.make_async_copy(al.at[:, s], out_al.at[:, s], osem.at[s])
+
+    def drain(s):
+        ring_end(
+            out(s, behind(rj, 1)), out(s, ahead(rj, 1)), out(s, ahead(rj, 2)), a_lower, a_upper,
+            AL + s * 6,
+        )
+        write_out(s).start()
+
     def in_order(t):
         return jnp.where(t == 0, 2, jnp.where(t == 1, 1, t + 1))
 
@@ -541,6 +550,14 @@
         def _():
             update_copy(d).start()
 
+        @pl.when(t == 1)
+        def _():
+            each(2, 4, pass_out)
+
+        @pl.when(t == 2)
+        def _():
+            each(0, 2, drain)
+
     def update_copy(d):
         peer = ahead(rj, d)
         return rcopy(ubf.at[peer], ugot.at[rj], UP + d - 1, {"rj": peer})
@@ -551,17 +568,7 @@
     keep = pltpu.make_async_copy(ugot, out_update, usem)
     keep.start()
 
-    def write_out(s):
-        return pltpu.make_async_copy(al.at[:, s], out_al.at[:, s], osem.at[s])
-
-    def drain(s):
-        ring_end(
-            out(s, behind(rj, 1)), out(s, ahead(rj, 1)), out(s, ahead(rj, 2)), a_lower, a_upper,
-            AL + s * 6,
-        )
-        write_out(s).start()
-
-    each(0, 4, drain)
+    each(2, 4, drain)
     each(0, 4, lambda s: ring_sent(out(s, rj), a_lower, a_upper, AL + s * 6))
     ring_sent(lb.at[:, x], q_lower, q_upper, LX)
     ring_sent(rb.at[:, rj], q_lower, q_upper, R4)

time: 76 us -> 76.6 us (level)
  no operation moved by 1% of the time
where the time goes in v10:
time: 76.6 us; the launch traced here: 76.3 us
  Pallas kernels  75.6 us (99%)
    pallas_call x1, Pallas kernels, on_device(): pl.pallas_call(kernel, out_shape=(jax.ShapeDtypeStruct((4, 4, 128, 256),...  73.2 us
    pallas_call x1, Pallas kernels, on_device(): pl.pallas_call(finish, out_shape=(jax.ShapeDtypeStruct((4, 4, 128, 256),...  2.43 us

profile of v10, /device:TPU:16, one launch (start us, length us, event | category | flops | bytes accessed | tf_op | source)
XLA Modules:
  0.0 76.3 jit_solution(331038228099320795)
XLA Ops:
  0.6 73.2 %shard_map.176 = (bf16[4,4,128,256]{3,2,1,0:T(8,128)(2,1)}, bf16[4,256,128]{2,1,0:T(8,128)(2,1)}) custom-call(bf16[16,128,256]{2,1,0:T(8,128)(2,1)} %hom.1, bf16[1024,128]{1,0:T(8,128)(2,1)} %bitcast.16, s32[4,128]{1,0:T(4,128)} %bitcast.27, s32[256]{0:T(256)} %rows_in.1, f32[1,256]{1,0:T(1,128)} %bitcast.29, bf16[64,256]{1,0:T(8,128)(2,1)} %bitcast.21, ...), custom_call_target="tpu_custom_call" | custom-call | flops 4000000000 | bytes 4000000 | tf_op jit(solution)/shard_map/pallas_call | solution.py:636
  73.8 2.4 %shard_map.177 = (bf16[4,4,128,256]{3,2,1,0:T(8,128)(2,1)}, bf16[1024,128]{1,0:T(8,128)(2,1)}) custom-call(bf16[4,4,128,256]{3,2,1,0:T(8,128)(2,1)} %get-tuple-element.6.al_in, bf16[4,256,128]{2,1,0:T(8,128)(2,1)} %get-tuple-element.7.update_in, bf16[1024,128]{1,0:T(8,128)(2,1)} %bitcast.17, s32[2,128]{1,0:T(2,128)} %bitcast.18), custom_call_target="tpu_custom_call" | custom-call | tf_op jit(solution)/shard_map/pallas_call | solution.py:717

commit v11 on v9

--- a/solution.py
+++ b/solution.py
@@ -9,8 +9,8 @@
 BF = jnp.bfloat16
 NT = (((1,), (1,)), ((), ()))
 
-SIZES = (8, 8, 4, 4, 6, 1, 1, 6, 6, 24, 1, 1, 6, 6, 3)
-RZ, XZ, XM, XF, WT, BA, BB, AX, BY, AL, LL, RR, LX, R4, UP = (
+SIZES = (8, 8, 4, 4, 6, 1, 1, 6, 6, 24, 1, 1, 6, 6, 3, 3)
+RZ, XZ, XM, XF, WT, BA, BB, AX, BY, AL, LL, RR, LX, R4, UP, WM = (
     sum(SIZES[:i]) for i in range(len(SIZES))
 )
 COUNT = sum(SIZES)
@@ -229,14 +229,18 @@
         rcopy(bg.at[1, zl, x, rj], bg.at[1, zl, x, rj], BB, in_zx(n)).start()
 
     each(1, 16, send_bias)
-    for s in range(4):
+    for s in range(2):
         send_x(s)
-    for s in range(4):
-        rcopy(xn.at[s, ri], xn.at[s, ri], XM + s, {"ri": mate}).start()
     for k in range(5, 10):
         local(k).wait()
-    w_lower, w_upper = first(160), second(160)
-    ring_start(wbuf.at[rj], w_lower, w_upper, WT, plus_y, minus_y)
+    w_row = pl.multiple_of(core * 160, 16)
+    w_other = pl.multiple_of(160 - core * 160, 16)
+    w_lower, w_upper = first(80), second(80)
+
+    def w_half(y):
+        return wbuf.at[y, pl.ds(w_row, 160)]
+
+    ring_start(w_half(rj), w_lower, w_upper, WT, plus_y, minus_y)
     for k in range(10, len(inward)):
         local(k).wait()
 
@@ -267,13 +271,13 @@
     b_lower, b_upper = first(2), second(2)
     ring_start(bg.at[0, :, x], b_lower, b_upper, AX, plus_x, minus_x)
     ring_start(bg.at[1, :, :, rj], b_lower, b_upper, BY, plus_y, minus_y)
+    for s in range(2, 4):
+        send_x(s)
+    for s in range(4):
+        rcopy(xn.at[s, ri], xn.at[s, ri], XM + s, {"ri": mate}).start()
     relay_x(0)
     relay_x(1)
-    ring_pass(
-        wbuf.at[behind(rj, 1)], wbuf.at[ahead(rj, 1)], w_lower, w_upper, WT, plus_y, minus_y
-    )
-    relay_x(2)
-    relay_x(3)
+    ring_pass(w_half(behind(rj, 1)), w_half(ahead(rj, 1)), w_lower, w_upper, WT, plus_y, minus_y)
     ring_pass(
         bg.at[0, :, behind(x, 1)], bg.at[0, :, ahead(x, 1)], b_lower, b_upper, AX, plus_x, minus_x
     )
@@ -282,9 +286,17 @@
         BY, plus_y, minus_y,
     )
 
+    relay_x(2)
+    relay_x(3)
+
     ring_end(
-        wbuf.at[behind(rj, 1)], wbuf.at[ahead(rj, 1)], wbuf.at[ahead(rj, 2)], w_lower, w_upper, WT
-    )
+        w_half(behind(rj, 1)), w_half(ahead(rj, 1)), w_half(ahead(rj, 2)), w_lower, w_upper, WT
+    )
+    for d in (1, 2, 3):
+        y = ahead(rj, d)
+        rcopy(w_half(y), w_half(y), WM + d - 1, {"ri": mate}).start()
+    for d in (1, 2, 3):
+        arrived(wbuf.at[ahead(rj, d), pl.ds(w_other, 160)], WM + d - 1)
 
     def weight(k):
         return wbuf[:, pl.ds(k * 64, 64), :].reshape(256, 256)
@@ -460,7 +472,9 @@
     each(0, 4, drain_head)
     left_here(fifteen, BA)
     left_here(fifteen, BB)
-    ring_sent(wbuf.at[rj], w_lower, w_upper, WT)
+    ring_sent(w_half(rj), w_lower, w_upper, WT)
+    for d in (1, 2, 3):
+        left_here(w_half(ahead(rj, d)), WM + d - 1)
     ring_sent(bg.at[0, :, x], b_lower, b_upper, AX)
     ring_sent(bg.at[1, :, :, rj], b_lower, b_upper, BY)
 

time: 76 us -> 77.6 us (1.021)
  Pallas kernels: 75 us -> 76.5 us
    pallas_call x1, Pallas kernels: 72.6 us -> 74.1 us  [on_device(): pl.pallas_call(kernel, out_shape=(jax.ShapeDtypeStruct((4, 4, 128, 256),...]
where the time goes in v11:
time: 77.6 us; the launch traced here: 77.2 us
  Pallas kernels  76.5 us (99%)
    pallas_call x1, Pallas kernels, on_device(): pl.pallas_call(kernel, out_shape=(jax.ShapeDtypeStruct((4, 4, 128, 256),...  74.1 us
    pallas_call x1, Pallas kernels, on_device(): pl.pallas_call(finish, out_shape=(jax.ShapeDtypeStruct((4, 4, 128, 256),...  2.43 us

profile of v11, /device:TPU:16, one launch (start us, length us, event | category | flops | bytes accessed | tf_op | source)
XLA Modules:
  0.0 77.2 jit_solution(2827827725121688342)
XLA Ops:
  0.6 74.1 %shard_map.176 = (bf16[4,4,128,256]{3,2,1,0:T(8,128)(2,1)}, bf16[4,256,128]{2,1,0:T(8,128)(2,1)}) custom-call(bf16[16,128,256]{2,1,0:T(8,128)(2,1)} %hom.1, bf16[1024,128]{1,0:T(8,128)(2,1)} %bitcast.16, s32[4,128]{1,0:T(4,128)} %bitcast.27, s32[256]{0:T(256)} %rows_in.1, f32[1,256]{1,0:T(1,128)} %bitcast.29, bf16[64,256]{1,0:T(8,128)(2,1)} %bitcast.21, ...), custom_call_target="tpu_custom_call" | custom-call | flops 4000000000 | bytes 4000000 | tf_op jit(solution)/shard_map/pallas_call | solution.py:643
  74.7 2.4 %shard_map.177 = (bf16[4,4,128,256]{3,2,1,0:T(8,128)(2,1)}, bf16[1024,128]{1,0:T(8,128)(2,1)}) custom-call(bf16[4,4,128,256]{3,2,1,0:T(8,128)(2,1)} %get-tuple-element.6.al_in, bf16[4,256,128]{2,1,0:T(8,128)(2,1)} %get-tuple-element.7.update_in, bf16[1024,128]{1,0:T(8,128)(2,1)} %bitcast.17, s32[2,128]{1,0:T(2,128)} %bitcast.18), custom_call_target="tpu_custom_call" | custom-call | tf_op jit(solution)/shard_map/pallas_call | solution.py:724
